TPU v7x, 128 devices: a whole 4x4x4 slice. The times are simulated.
128 devices in a mesh: orb: 4 (over y_lo, core), grid: 32 (over x, y_hi, z).
Axes of the slice: x: 4, y: 4 (y_hi: 2, y_lo: 2; y = y_hi * 2 + y_lo), z: 4, core: 2. Of those that a mesh axis runs over, the one named last changes fastest.
Arguments:
- orbitals: bfloat16 [8192, 49152], P('orb', 'grid'), may hold values from -7 to 7, as said below
- block_order: int32 [16], replicated, may hold values from 0 to 15, each once
Outputs:
- factor_rows: float32 [1024, 8192], P(None, 'orb')
- ortho: float32 [1024, 49152], P('orb', 'grid')
Inputs may be any that keep to these rules, and one draw needn't show every extreme that they name: `block_order`: each block number appears once. `orbitals`: orbitals are linearly independent and of order one.
All inputs are finite; a program needn't handle non-finite values.
Results may differ from a plain program's by a relative error of at most 0.0003.
Values may be sent and summed in bfloat16 or wider, within the bound.
A program may use at most 128 MiB of HBM per device.

v0:
```python
import jax
import jax.numpy as jnp
from jax import lax
from jax.sharding import PartitionSpec as P

B = 512
BPD = 4


def broadcast(value, axis, source):
    kept = jnp.where(lax.axis_index(axis) == source, value, 0).astype(value.dtype)
    return lax.psum(kept, axis)


def factor_pieces(diag_tiles):
    identity = jnp.eye(B, dtype=jnp.float32)
    first_chol = jnp.linalg.cholesky(diag_tiles[:B, :B])
    first_inv = jax.scipy.linalg.solve_triangular(first_chol, identity, lower=True)
    coupling = jnp.dot(first_inv, diag_tiles[:B, B:], precision=lax.Precision.HIGHEST)
    schur_block = diag_tiles[B:, B:] - jnp.dot(
        coupling.T, coupling, precision=lax.Precision.HIGHEST
    )
    second_chol = jnp.linalg.cholesky(schur_block)
    second_inv = jax.scipy.linalg.solve_triangular(second_chol, identity, lower=True)
    lower_part = -jnp.dot(
        jnp.dot(second_inv, coupling.T, precision=lax.Precision.HIGHEST),
        first_inv,
        precision=lax.Precision.HIGHEST,
    )
    empty_tile = jnp.zeros((B, B), jnp.float32)
    mixing = jnp.concatenate(
        [jnp.concatenate([first_inv, empty_tile], 1), jnp.concatenate([lower_part, second_inv], 1)],
        0,
    )
    return (first_inv, coupling, second_inv, mixing)


def triangular_rows(gram_rows, first_inv, coupling, second_inv, column_blocks, first_block):
    upper_first = jnp.dot(first_inv, gram_rows[:B], precision=lax.Precision.HIGHEST)
    reduced = gram_rows[B:] - jnp.dot(coupling.T, upper_first, precision=lax.Precision.HIGHEST)
    upper_second = jnp.dot(second_inv, reduced, precision=lax.Precision.HIGHEST)
    upper_second = jnp.where(
        (column_blocks == first_block)[None, :], jnp.float32(0.0), upper_second
    )
    return jnp.concatenate([upper_first, upper_second], 0)


def local(orbitals, block_order):
    own_index = lax.axis_index("orb")
    local_cols = orbitals.shape[0]
    cells = orbitals.shape[1] * lax.axis_size("grid")
    first_block = block_order[0]
    second_block = block_order[1]

    def fetch_block(block_index):
        piece = lax.dynamic_slice_in_dim(orbitals, block_index % BPD * B, B, 0)
        return broadcast(piece, "orb", block_index // BPD)

    panel = jnp.concatenate([fetch_block(first_block), fetch_block(second_block)], 0)
    local_gram = lax.dot_general(
        panel, orbitals, (((1,), (1,)), ((), ())), preferred_element_type=jnp.float32
    )
    summed = lax.psum(local_gram, "grid")
    gram_all = summed * (1.0 / cells)

    def pick_tile(block_index):
        columns = lax.dynamic_slice_in_dim(gram_all, block_index % BPD * B, B, 1)
        return jnp.where(block_index // BPD == own_index, columns, jnp.float32(0.0))

    diag_tiles = lax.psum(
        jnp.concatenate([pick_tile(first_block), pick_tile(second_block)], 1), "orb"
    )
    first_inv, coupling, second_inv, mixing = factor_pieces(diag_tiles)
    column_blocks = (own_index * local_cols + jnp.arange(local_cols, dtype=jnp.int32)) // B
    factor_rows = triangular_rows(
        gram_all, first_inv, coupling, second_inv, column_blocks, first_block
    )
    rows_dev = 2 * B // lax.axis_size("orb")
    mixing_rows = lax.dynamic_slice_in_dim(mixing, own_index * rows_dev, rows_dev, 0)
    ortho = jnp.dot(mixing_rows, panel.astype(jnp.float32), precision=lax.Precision.HIGHEST)
    return (factor_rows, ortho)


def solution(mesh):
    return jax.shard_map(
        local,
        mesh=mesh,
        in_specs=(P("orb", "grid"), P()),
        out_specs=(P(None, "orb"), P("orb", "grid")),
        check_vma=False,
    )
```

profile of v0, /device:TPU:0, one launch (start us, length us, event | category | flops | bytes accessed | tf_op | source)
XLA Modules:
  0.0 944.5 jit_solution(12815428012536219016)
XLA Ops:
  13.9 4.1 dynamic-slice_select_fusion.2
  18.0 77.2 %all-reduce.11.cloned.1.call-done = (bf16[512,1536]{1,0:T(8,128)(2,1)}, bf16[512,1536]{1,0:T(8,128)(2,1)}) async-done(((bf16[512,1536]{1,0:T(8,128)(2,1)}, bf16[512,1536]{1,0:T(8,128)(2,1)}), (bf16[512,1536]{1,0:T(8,128)(2,1)}, bf16[512,1536]{1,0:T(8,128)(2,1)})) %all-reduce.11.cloned.1.call-update) | async-done | bytes 3145744 | tf_op jit(solution)/shard_map/psum | solution.py:12
  95.2 1.7 constant_dynamic-update-slice_fusion.1
  96.9 1.8 constant_dynamic-update-slice_fusion
  99.0 8.9 fusion.94
  108.1 386.3 %all-reduce.7.cloned.1.call-done = f32[1024,2048]{0,1:T(8,128)} async-done(((f32[1024,2048]{0,1:T(8,128)}), f32[1024,2048]{0,1:T(8,128)}) %all-reduce.7.cloned.1.call-update) | async-done | bytes 8388624 | tf_op jit(solution)/shard_map/psum | solution.py:63
  494.5 4.4 broadcast_multiply_fusion
  499.3 2.9 copy-done
  502.3 2.5 pad_maximum_fusion.1
  505.6 91.0 %all-reduce.9.cloned.1.call-done = f32[1024,1024]{0,1:T(8,128)} async-done(((f32[1024,1024]{0,1:T(8,128)}), f32[1024,1024]{0,1:T(8,128)}) %all-reduce.9.cloned.1.call-update) | async-done | bytes 4194320 | tf_op jit(solution)/shard_map/psum | solution.py:70
  598.2 1.4 fusion.17
  599.6 11.7 %cholesky.286 = f32[128,128]{1,0:T(8,128)S(1)} custom-call(f32[128,128]{1,0:T(8,128)S(1)} %cholesky.426), custom_call_target="Cholesky" | custom-call | tf_op jit(solution)/shard_map/jit(cholesky)/cholesky | solution.py:17
  611.4 9.8 %custom-call.27 = f32[1,128,128]{1,2,0:T(8,128)S(1)} custom-call(f32[1,128,128]{2,1,0:T(8,128)S(1)} %get-tuple-element.65), custom_call_target="InvertDiagBlocksLowerTriangular" | custom-call | tf_op jit(solution)/shard_map/jit(cholesky)/cholesky | solution.py:17
  622.0 11.9 %cholesky.305 = f32[128,128]{1,0:T(8,128)S(1)} custom-call(f32[128,128]{1,0:T(8,128)S(1)} %cholesky.430), custom_call_target="Cholesky" | custom-call | tf_op jit(solution)/shard_map/jit(cholesky)/cholesky | solution.py:17
  633.9 9.8 %custom-call.28 = f32[1,128,128]{1,2,0:T(8,128)S(1)} custom-call(f32[1,128,128]{2,1,0:T(8,128)S(1)} %get-tuple-element.62), custom_call_target="InvertDiagBlocksLowerTriangular" | custom-call | tf_op jit(solution)/shard_map/jit(cholesky)/cholesky | solution.py:17
  644.4 11.7 %cholesky.326 = f32[128,128]{1,0:T(8,128)S(1)} custom-call(f32[128,128]{1,0:T(8,128)S(1)} %cholesky.435), custom_call_target="Cholesky" | custom-call | tf_op jit(solution)/shard_map/jit(cholesky)/cholesky | solution.py:17
  656.9 9.8 %custom-call.29 = f32[1,128,128]{1,2,0:T(8,128)S(1)} custom-call(f32[1,128,128]{2,1,0:T(8,128)S(1)} %get-tuple-element.59), custom_call_target="InvertDiagBlocksLowerTriangular" | custom-call | tf_op jit(solution)/shard_map/jit(cholesky)/cholesky | solution.py:17
  667.3 12.1 %cholesky.343 = f32[128,128]{1,0:T(8,128)S(1)} custom-call(f32[128,128]{1,0:T(8,128)S(1)} %convolution_subtract_fusion.12), custom_call_target="Cholesky" | custom-call | tf_op jit(solution)/shard_map/jit(cholesky)/cholesky | solution.py:17
  683.6 8.4 while.4
  691.9 39.3 %custom-call.30 = f32[4,128,128]{1,2,0:T(8,128)S(1)} custom-call(f32[4,128,128]{2,1,0:T(8,128)S(1)} %get-tuple-element.18), custom_call_target="InvertDiagBlocksLowerTriangular" | custom-call | tf_op jit(solution)/shard_map/jit(_solve_triangular)/triangular_solve | solution.py:18
  735.5 10.4 %fusion.1 = f32[512,2048]{1,0:T(8,128)} fusion(f32[1024,2048]{0,1:T(8,128)} %copy-done, f32[128,512]{1,0:T(8,128)S(1)} %fusion.65, f32[128,512]{1,0:T(8,128)S(1)} %fusion.66, f32[128,512]{1,0:T(8,128)S(1)} %fusion.68, f32[128,512]{1,0:T(8,128)S(1)} %fusion.43), kind=kOutput, calls=%fused_computation.8 | convolution fusion | flops 6443237376 | bytes 9437184 | tf_op jit(solution)/shard_map/dot_general | solution.py:39
  745.9 1.9 fusion.14
  747.7 2.9 convolution_subtract_fusion
  750.6 2.5 copy.7
  753.2 1.8 fusion.16
  755.9 11.7 %cholesky.358 = f32[128,128]{1,0:T(8,128)S(1)} custom-call(f32[128,128]{1,0:T(8,128)S(1)} %cholesky.439), custom_call_target="Cholesky" | custom-call | tf_op jit(solution)/shard_map/jit(cholesky)/cholesky | solution.py:23
  768.3 9.8 %custom-call.31 = f32[1,128,128]{1,2,0:T(8,128)S(1)} custom-call(f32[1,128,128]{2,1,0:T(8,128)S(1)} %get-tuple-element.55), custom_call_target="InvertDiagBlocksLowerTriangular" | custom-call | tf_op jit(solution)/shard_map/jit(cholesky)/cholesky | solution.py:23
  779.2 1.9 constant_dynamic-update-slice_fusion.2
  782.4 12.1 %cholesky.377 = f32[128,128]{1,0:T(8,128)S(1)} custom-call(f32[128,128]{1,0:T(8,128)S(1)} %cholesky.443), custom_call_target="Cholesky" | custom-call | tf_op jit(solution)/shard_map/jit(cholesky)/cholesky | solution.py:23
  795.9 9.8 %custom-call.32 = f32[1,128,128]{1,2,0:T(8,128)S(1)} custom-call(f32[1,128,128]{2,1,0:T(8,128)S(1)} %get-tuple-element.52), custom_call_target="InvertDiagBlocksLowerTriangular" | custom-call | tf_op jit(solution)/shard_map/jit(cholesky)/cholesky | solution.py:23
  808.1 11.7 %cholesky.398 = f32[128,128]{1,0:T(8,128)S(1)} custom-call(f32[128,128]{1,0:T(8,128)S(1)} %cholesky.448), custom_call_target="Cholesky" | custom-call | tf_op jit(solution)/shard_map/jit(cholesky)/cholesky | solution.py:23
  821.1 9.8 %custom-call.33 = f32[1,128,128]{1,2,0:T(8,128)S(1)} custom-call(f32[1,128,128]{2,1,0:T(8,128)S(1)} %get-tuple-element.49), custom_call_target="InvertDiagBlocksLowerTriangular" | custom-call | tf_op jit(solution)/shard_map/jit(cholesky)/cholesky | solution.py:23
  831.8 1.6 convolution_subtract_fusion.11
  833.4 11.7 %cholesky.415 = f32[128,128]{1,0:T(8,128)S(1)} custom-call(f32[128,128]{1,0:T(8,128)S(1)} %convolution_subtract_fusion.11), custom_call_target="Cholesky" | custom-call | tf_op jit(solution)/shard_map/jit(cholesky)/cholesky | solution.py:23
  848.9 2.3 select_select_fusion
  851.3 11.4 %while.5 = (s32[]{:T(128)}, f32[512,512]{1,0:T(8,128)}, s32[4,2]{0,1:T(2,128)S(1)}, f32[4,128,128]{2,1,0:T(8,128)S(1)}, s32[]{:T(128)}) while((s32[]{:T(128)}, f32[512,512]{1,0:T(8,128)}, s32[4,2]{0,1:T(2,128)S(1)}, f32[4,128,128]{2,1,0:T(8,128)S(1)}, s32[]{:T(128)}) %tuple.71), condition=%wide.while_cond.clone, body=%wide.while_body.clone.sunk | while | flops 2 | bytes 131189 | solution.py:24
  851.9 2.2 bitcast_dynamic-update-slice_fusion.5
  854.8 2.2 bitcast_dynamic-update-slice_fusion.5
  857.7 2.2 bitcast_dynamic-update-slice_fusion.5
  860.5 2.2 bitcast_dynamic-update-slice_fusion.5
  863.4 40.1 %custom-call.34 = f32[4,128,128]{1,2,0:T(8,128)S(1)} custom-call(f32[4,128,128]{2,1,0:T(8,128)} %copy-done.7), custom_call_target="InvertDiagBlocksLowerTriangular" | custom-call | tf_op jit(solution)/shard_map/jit(_solve_triangular)/triangular_solve | solution.py:24
  907.4 1.7 convolution_subtract_fusion.5
  909.5 1.9 fusion.29
  911.4 1.8 convolution_negate_fusion
  913.3 7.0 fusion.95
  920.3 6.9 fusion.3
  927.2 4.0 pad_maximum_fusion
  931.2 6.5 fusion.6
  (104 shorter events, 40.2 us)
Async XLA Ops:
  7.2 88.1 %all-reduce.11.cloned.1.call-start = ((), (), s32[]{:S(2)}) async-start(), calls=%async_computation.2 | async-start | bytes 6291456 | tf_op jit(solution)/shard_map/psum | solution.py:12
  18.0 476.5 %all-reduce.7.cloned.1.call-start = ((), (), s32[]{:S(2)}) async-start(), calls=%async_computation | async-start | bytes 16777216 | tf_op jit(solution)/shard_map/psum | solution.py:63
  95.2 3.7 copy-start.4
  99.0 8.9 copy-start.6
  107.9 488.6 %all-reduce.9.cloned.1.call-start = ((), (), s32[]{:S(2)}) async-start(), calls=%async_computation.1 | async-start | bytes 8388608 | tf_op jit(solution)/shard_map/psum | solution.py:70
  498.9 3.4 copy-start
  735.5 10.4 %copy-start.2 = (f32[1024,1024]{0,1:T(8,128)S(1)}, f32[1024,1024]{0,1:T(8,128)}, u32[]{:S(2)}) copy-start(f32[1024,1024]{0,1:T(8,128)} %all-reduce.9.cloned.1.call-done) | copy-start | bytes 12582916
  754.9 1.0 copy-start.3
  862.7 0.7 copy-start.7
  907.3 5.9 copy-start.1
  909.5 10.8 %slice-start = ((s8[8388608]{0:T(1024)(128)(4,1)}), s8[4194304]{0:T(1024)(128)(4,1)S(1)}, s32[]{:S(2)}) async-start(s8[8388608]{0:T(1024)(128)(4,1)} %bitcast.107), calls=%async_computation.3 | async-start | bytes 8388608
  913.2 7.1 slice-start.1
  927.2 4.0 copy-start.5
Sparse Core Ops, SparseCore 0:
  18.1 77.0 all-reduce.10
  108.0 386.3 all-reduce.6
  504.9 91.6 all-reduce.8
where the time goes:
time: 949 us; the launch traced here: 944 us
  waiting for transfers between devices  555 us (58%)
  other arithmetic  263 us (28%)
  matrix products  67 us (7%)
  local copies, waits for them, and re-layouts  34.7 us (4%)
  between operations  25 us (3%)
    psum x1, waiting for transfers between devices, local(): summed = lax.psum(local_gram, 'grid')  386 us
    psum x1, waiting for transfers between devices, local(): lax.psum(jnp.concatenate([pick_tile(first_block), pick_tile(second_block)...  91 us
    another operation x15, other arithmetic, factor_pieces(): second_chol = jnp.linalg.cholesky(schur_block)  81.3 us
    another operation x14, other arithmetic, factor_pieces(): first_chol = jnp.linalg.cholesky(diag_tiles[:B, :B])  79.1 us
    psum x1, waiting for transfers between devices, broadcast(): return lax.psum(kept, axis)  77.2 us
    another operation x2, other arithmetic, factor_pieces(): jax.scipy.linalg.solve_triangular(second_chol, identity, lower=True)  42.5 us
    another operation x4, other arithmetic, factor_pieces(): jax.scipy.linalg.solve_triangular(first_chol, identity, lower=True)  40.5 us
  transfers between devices with their start and end apart: 3, of which 3 were waited for; matrix products, arithmetic and copies ran while one was open for 0% of the time, Pallas kernels for 0%

commit v1 on v0

v1 whole, which is shorter than its diff:
```python
import jax
import jax.numpy as jnp
from jax import lax
from jax.experimental import pallas as pl
from jax.experimental.pallas import tpu as pltpu
from jax.sharding import PartitionSpec as P

B = 512
BPD = 4
BLK = 128
SUB = 8
HI = lax.Precision.HIGHEST


def invert_block(block_ref, out_ref):
    shape = (SUB, BLK)
    lane = lax.broadcasted_iota(jnp.int32, shape, 1)
    row = lax.broadcasted_iota(jnp.int32, shape, 0)
    count = BLK // SUB
    tiles = [block_ref[SUB * i : SUB * i + SUB, :] for i in range(count)]
    for c in range(count):
        low = SUB * c
        here = jnp.logical_and(lane >= low, lane < low + SUB)
        pivot = tiles[c]
        column = [jnp.broadcast_to(pivot[:, low + m : low + m + 1], shape) for m in range(SUB)]
        a = {}
        for m in range(SUB):
            for i in range(m, SUB):
                a[i, m] = jnp.broadcast_to(column[m][i : i + 1, :], shape)
        marked = jnp.where(here, (lane - low == row).astype(jnp.float32), pivot)
        y = [jnp.broadcast_to(marked[k : k + 1, :], shape) for k in range(SUB)]
        t = {}
        for m in range(SUB):
            r = lax.rsqrt(a[m, m])
            for i in range(m + 1, SUB):
                a[i, m] = a[i, m] * r
            y[m] = y[m] * r
            for k in range(m):
                t[m, k] = t[m, k] * r
            t[m, m] = r
            for j in range(m + 1, SUB):
                for i in range(j, SUB):
                    a[i, j] = a[i, j] - a[i, m] * a[j, m]
            for i in range(m + 1, SUB):
                y[i] = y[i] - a[i, m] * y[m]
                for k in range(m):
                    t[i, k] = t[i, k] - a[i, m] * t[m, k]
                t[i, m] = -(a[i, m] * r)
        tile = y[0]
        for i in range(1, SUB):
            tile = jnp.where(row == i, y[i], tile)
        out_ref[low : low + SUB, :] = jnp.where(lane < low + SUB, tile, 0.0)
        if c == count - 1:
            break
        z = []
        for k in range(SUB):
            acc = t[k, k] * y[k]
            for i in range(k + 1, SUB):
                acc = acc + t[i, k] * y[i]
            z.append(acc)
        for r in range(c + 1, count):
            terms = [jnp.broadcast_to(tiles[r][:, low + m : low + m + 1], shape) * z[m] for m in range(SUB)]
            while len(terms) > 1:
                terms = [terms[i] + terms[i + 1] for i in range(0, len(terms), 2)]
            tiles[r] = jnp.where(here, 0.0, tiles[r]) - terms[0]


def inverse_factor_kernel(g_ref, out_ref, work, block, inv):
    n = g_ref.shape[0]
    count = n // BLK
    work[...] = g_ref[...]
    column = lax.broadcasted_iota(jnp.int32, (BLK, n), 1)

    def step(k, carry):
        start = pl.multiple_of(k * BLK, BLK)
        here = pl.ds(start, BLK)
        block[...] = work[here, here]
        invert_block(block, inv)
        t = inv[...]
        row = jnp.dot(t, work[here, :], precision=HI, preferred_element_type=jnp.float32)
        out_ref[here, :] = jnp.where(column < start, row, 0.0)
        out_ref[here, here] = t
        work[here, :] = row
        work[here, here] = t

        def update(i, carry):
            rows = pl.ds(pl.multiple_of(i * BLK, BLK), BLK)
            u = work[here, rows]
            work[rows, here] = jnp.zeros((BLK, BLK), jnp.float32)
            work[rows, :] -= lax.dot_general(
                u, work[here, :], (((0,), (0,)), ((), ())), precision=HI, preferred_element_type=jnp.float32
            )
            return carry

        return lax.fori_loop(k + 1, count, update, carry)

    lax.fori_loop(0, count, step, 0)


def inverse_factor(g):
    n = g.shape[0]
    return pl.pallas_call(
        inverse_factor_kernel,
        out_shape=jax.ShapeDtypeStruct((n, n), jnp.float32),
        in_specs=[pl.BlockSpec(memory_space=pltpu.VMEM)],
        out_specs=pl.BlockSpec(memory_space=pltpu.VMEM),
        scratch_shapes=[
            pltpu.VMEM((n, n), jnp.float32),
            pltpu.VMEM((BLK, BLK), jnp.float32),
            pltpu.VMEM((BLK, BLK), jnp.float32),
        ],
        compiler_params=pltpu.CompilerParams(vmem_limit_bytes=40 << 20),
    )(g)


CELLS = 49152
ROWS = 2 * B
MAIN = 1280
WIDE = 1024
RING = 4
MESH = pl.DeviceIdType.MESH


def gram_kernel(cand_ref, orb_ref, panel_out, gram_out, diag_out,
                panel, merged, from_core, from_chip, gram, first, second, third, diag,
                panel_send, panel_recv, send, recv, free, local):
    o = lax.axis_index("orb")
    g = lax.axis_index("grid")
    core = o % 2
    mate = o + 1 - 2 * core
    across = (o + 2) % 4
    x = g // 8
    y = (g // 4) % 2
    z = g % 4
    x_next = ((x + 1) % RING) * 8 + y * 4 + z
    x_prev = ((x + 3) % RING) * 8 + y * 4 + z
    z_next = x * 8 + y * 4 + (z + 1) % RING
    z_prev = x * 8 + y * 4 + (z + 3) % RING
    y_mate = x * 8 + (1 - y) * 4 + z

    barrier = pltpu.get_barrier_semaphore()
    for other in (mate, across):
        pl.semaphore_signal(barrier, inc=1, device_id={"orb": other}, device_id_type=MESH)
    for other in (x_next, x_prev, z_next, z_prev, y_mate):
        pl.semaphore_signal(barrier, inc=1, device_id={"grid": other}, device_id_type=MESH)
    pl.semaphore_wait(barrier, 7)

    piece = B // PIECES
    mine = core * B
    theirs = (1 - core) * B

    def part(start, j):
        return pl.ds(pl.multiple_of(start + j * piece, piece), piece)

    def orb_copy(src, dst, other, index):
        return pltpu.make_async_remote_copy(
            src_ref=src, dst_ref=dst, send_sem=panel_send.at[index], recv_sem=panel_recv.at[index],
            device_id={"orb": other}, device_id_type=MESH)

    a = [orb_copy(cand_ref.at[part(theirs, j)], from_core.at[j], mate, j) for j in range(PIECES)]
    b = [orb_copy(merged.at[j], from_chip.at[j], across, PIECES + j) for j in range(PIECES)]
    c = [orb_copy(panel.at[part(mine, j)], panel.at[part(mine, j)], mate, 2 * PIECES + j) for j in range(PIECES)]
    for copy in a:
        copy.start()
    for j in range(PIECES):
        a[j].wait_recv()
        merged[j] = cand_ref[part(mine, j), :] + from_core[j]
        b[j].start()
    for j in range(PIECES):
        b[j].wait_recv()
        panel[part(mine, j), :] = merged[j] + from_chip[j]
        c[j].start()
    for j in range(PIECES):
        c[j].wait_recv()
    for copy in a + b + c:
        copy.wait_send()
    save_panel = pltpu.make_async_copy(panel, panel_out, local.at[0])
    save_panel.start()

    contract = (((1,), (1,)), ((), ()))
    tile = 256

    for h in range(2):
        def column(n, carry, h=h):
            at = pl.multiple_of(n * tile, tile)
            gram[h, :ROWS, pl.ds(at, tile)] = lax.dot_general(
                panel[...], orb_ref[pl.ds(h * WIDE + at, tile), :], contract, preferred_element_type=jnp.float32)
            gram[h, ROWS:, pl.ds(at, tile)] = lax.dot_general(
                panel[pl.ds(pl.multiple_of(core * B + h * 256, 256), 256), :], panel[pl.ds(at, tile), :],
                contract, preferred_element_type=jnp.float32)
            return carry

        lax.fori_loop(0, WIDE // tile, column, 0)

    count = [0]
    started = []

    def grid_copy(src, dst, other):
        index = count[0]
        count[0] += 1
        copy = pltpu.make_async_remote_copy(
            src_ref=src, dst_ref=dst, send_sem=send.at[index], recv_sem=recv.at[index],
            device_id={"grid": other}, device_id_type=MESH)
        copy.start()
        started.append(copy)
        return copy

    def sent(*copies):
        for copy in copies:
            copy.wait_send()
            started[:] = [other for other in started if other is not copy]

    def reduce_ring(h, p, following, previous, base, size, slots, spare):
        half = size // 2

        def rows(q, which):
            return pl.ds(pl.multiple_of(base + ((p + q) % RING) * size + which * half, 8), half)

        data = gram.at[h]
        far_f = grid_copy(data.at[rows(2, 0)], slots.at[0], following)
        far_b = grid_copy(data.at[rows(2, 1)], slots.at[1], previous)
        near_f = grid_copy(data.at[rows(1, 1)], slots.at[2], following)
        near_b = grid_copy(data.at[rows(3, 0)], slots.at[3], previous)
        yield
        far_f.wait_recv()
        slots[0] = slots[0] + gram[h, rows(1, 0), :]
        sum_f = grid_copy(slots.at[0], slots.at[4], following)
        far_b.wait_recv()
        slots[1] = slots[1] + gram[h, rows(3, 1), :]
        sum_b = grid_copy(slots.at[1], slots.at[5], previous)
        yield
        near_f.wait_recv()
        near_b.wait_recv()
        sum_f.wait_recv()
        gram[h, rows(0, 0), :] = gram[h, rows(0, 0), :] + (slots[3] + slots[4])
        sum_b.wait_recv()
        gram[h, rows(0, 1), :] = gram[h, rows(0, 1), :] + (slots[2] + slots[5])
        sent(far_f, far_b, near_f, near_b)
        for other in (following, previous):
            pl.semaphore_signal(spare, inc=1, device_id={"grid": other}, device_id_type=MESH)

    def gather_ring(h, p, following, previous, base, size, spare):
        half = size // 2
        data = gram.at[h]

        def rows(q, which):
            return data.at[pl.ds(pl.multiple_of(base + ((p + q) % RING) * size + which * half, 8), half)]

        own = data.at[pl.ds(pl.multiple_of(base + p * size, 8), size)]
        pl.semaphore_wait(spare, 2)
        near_f = grid_copy(own, own, following)
        near_b = grid_copy(own, own, previous)
        yield
        near_f.wait_recv()
        far_f = grid_copy(rows(3, 0), rows(3, 0), following)
        near_b.wait_recv()
        far_b = grid_copy(rows(1, 1), rows(1, 1), previous)
        yield
        far_f.wait_recv()
        far_b.wait_recv()

    def all_reduce(h, p, following, previous, q, q_following, q_previous, slots):
        one = MAIN // RING
        two = one // RING
        three = two // 2
        base = p * one
        low = base + q * two
        yield from reduce_ring(h, p, following, previous, 0, one, slots[0], free.at[h, 0])
        yield from reduce_ring(h, q, q_following, q_previous, base, two, slots[1], free.at[h, 1])
        own = pl.ds(pl.multiple_of(low + y * three, 8), three)
        rest = pl.ds(pl.multiple_of(low + (1 - y) * three, 8), three)
        swap = grid_copy(gram.at[h, rest], slots[2], y_mate)
        yield
        swap.wait_recv()
        gram[h, own, :] = gram[h, own, :] + slots[2][...]
        share = grid_copy(gram.at[h, own], slots[3], y_mate)
        yield
        share.wait_recv()
        sent(swap)
        gram[h, rest, :] = slots[3][...]
        yield from gather_ring(h, q, q_following, q_previous, base, two, free.at[h, 1])
        yield from gather_ring(h, p, following, previous, 0, one, free.at[h, 0])

    runs = [
        all_reduce(0, x, x_next, x_prev, z, z_next, z_prev, [first.at[0], second.at[0], third.at[0], third.at[1]]),
        all_reduce(1, z, z_next, z_prev, x, x_next, x_prev, [first.at[1], second.at[1], third.at[2], third.at[3]]),
    ]
    while runs:
        for run in list(runs):
            try:
                next(run)
            except StopIteration:
                runs.remove(run)

    saves = []
    shares = []
    for h in range(2):
        shares.append(orb_copy(gram.at[h, pl.ds(ROWS, 256)], diag.at[h], mate, 3 * PIECES + h))
        shares[-1].start()
        saves.append(pltpu.make_async_copy(
            gram.at[h, pl.ds(0, ROWS)], gram_out.at[:, pl.ds(h * WIDE, WIDE)], local.at[1 + h]))
        saves.append(pltpu.make_async_copy(
            gram.at[h, pl.ds(ROWS, 256)], diag_out.at[pl.ds(pl.multiple_of(core * B + h * 256, 256), 256)],
            local.at[3 + h]))
    for save in saves:
        save.start()
    for h in range(2):
        shares[h].wait_recv()
        save = pltpu.make_async_copy(
            diag.at[h], diag_out.at[pl.ds(pl.multiple_of((1 - core) * B + h * 256, 256), 256)], local.at[5 + h])
        save.start()
        saves.append(save)
    for copy in started + shares:
        copy.wait_send()
    save_panel.wait()
    for save in saves:
        save.wait()


PIECES = 4


def gram_sums(cand, orbitals):
    cells = orbitals.shape[1]
    f32 = jnp.float32
    any_space = pl.BlockSpec(memory_space=pl.ANY)
    return pl.pallas_call(
        gram_kernel,
        out_shape=(
            jax.ShapeDtypeStruct((ROWS, cells), jnp.bfloat16),
            jax.ShapeDtypeStruct((ROWS, 2 * WIDE), f32),
            jax.ShapeDtypeStruct((ROWS, ROWS), f32),
        ),
        in_specs=[pl.BlockSpec(memory_space=pltpu.VMEM)] * 2,
        out_specs=(any_space,) * 3,
        scratch_shapes=[
            pltpu.VMEM((ROWS, cells), jnp.bfloat16),
            pltpu.VMEM((PIECES, B // PIECES, cells), jnp.bfloat16),
            pltpu.VMEM((PIECES, B // PIECES, cells), jnp.bfloat16),
            pltpu.VMEM((PIECES, B // PIECES, cells), jnp.bfloat16),
            pltpu.VMEM((2, MAIN, WIDE), f32),
            pltpu.VMEM((2, 6, MAIN // 8, WIDE), f32),
            pltpu.VMEM((2, 6, MAIN // 32, WIDE), f32),
            pltpu.VMEM((4, MAIN // 32, WIDE), f32),
            pltpu.VMEM((2, 256, WIDE), f32),
            pltpu.SemaphoreType.DMA((3 * PIECES + 2,)),
            pltpu.SemaphoreType.DMA((3 * PIECES + 2,)),
            pltpu.SemaphoreType.DMA((44,)),
            pltpu.SemaphoreType.DMA((44,)),
            pltpu.SemaphoreType.REGULAR((2, 2)),
            pltpu.SemaphoreType.DMA((7,)),
        ],
        compiler_params=pltpu.CompilerParams(
            collective_id=0, has_side_effects=True, vmem_limit_bytes=56 << 20),
    )(cand, orbitals)


def local(orbitals, block_order):
    own_index = lax.axis_index("orb")
    local_cols = orbitals.shape[0]
    first_block = block_order[0]
    second_block = block_order[1]

    def candidate(block_index):
        piece = lax.dynamic_slice_in_dim(orbitals, block_index % BPD * B, B, 0)
        return jnp.where(block_index // BPD == own_index, piece, 0).astype(piece.dtype)

    cand = jnp.concatenate([candidate(first_block), candidate(second_block)], 0)
    panel, gram, diag = gram_sums(cand, orbitals)
    scale = jnp.float32(1.0 / CELLS)
    mixing = inverse_factor(diag * scale)
    column_blocks = (own_index * local_cols + jnp.arange(local_cols, dtype=jnp.int32)) // B
    scaled = mixing * scale
    upper_first = jnp.dot(scaled[:B, :B], gram[:B], precision=lax.Precision.HIGH)
    upper_second = jnp.dot(scaled[B:], gram, precision=lax.Precision.HIGH)
    upper_second = jnp.where((column_blocks == first_block)[None, :], jnp.float32(0.0), upper_second)
    factor_rows = jnp.concatenate([upper_first, upper_second], 0)
    rows_dev = ROWS // lax.axis_size("orb")
    mixing_rows = lax.dynamic_slice_in_dim(mixing, own_index * rows_dev, rows_dev, 0)
    high = lax.reduce_precision(mixing_rows, 8, 7)
    low = (mixing_rows - high).astype(jnp.bfloat16)
    ortho = jnp.dot(high.astype(jnp.bfloat16), panel, preferred_element_type=jnp.float32) + jnp.dot(
        low, panel, preferred_element_type=jnp.float32)
    return (factor_rows, ortho)


def solution(mesh):
    return jax.shard_map(
        local,
        mesh=mesh,
        in_specs=(P("orb", "grid"), P()),
        out_specs=(P(None, "orb"), P("orb", "grid")),
        check_vma=False,
    )
```

time: 949 us -> 291 us (0.31)
  waiting for transfers between devices: 555 us -> 0 us
  Pallas kernels: 0 us -> 254 us
  other arithmetic: 263 us -> 12.9 us
  matrix products: 67 us -> 14.2 us
  local copies, waits for them, and re-layouts: 34.7 us -> 2.73 us
  between operations: 25 us -> 5.98 us
    psum x3 -> x0, waiting for transfers between devices: 554 us -> none  [the longest x1 386 us: local(): summed = lax.psum(local_gram, 'grid')]
    pallas_call x0 -> x2, Pallas kernels: none -> 254 us  [the longest x1 192 us: gram_sums(): pl.pallas_call(gram_kernel, out_shape=(jax.ShapeDtypeStruct((ROWS, cells)...]
    another operation x35 -> x0, other arithmetic: 243 us -> none  [the longest x15 81.3 us: factor_pieces(): second_chol = jnp.linalg.cholesky(schur_block)]
    dot_general x9 -> x4, matrix products: 48.2 us -> 14.2 us  [the longest x1 7.38 us: local(): upper_second = jnp.dot(scaled[B:], gram, precision=lax.Precision.HIGH)]
    another operation x35 -> x0, local copies, waits for them, and re-layouts: 20.9 us -> none  [the longest x12 11.3 us: factor_pieces(): jax.scipy.linalg.solve_triangular(second_chol, identity, lower=True)]
    another operation x26 -> x0, matrix products: 18.8 us -> none  [the longest x6 7.92 us: factor_pieces(): second_chol = jnp.linalg.cholesky(schur_block)]
  transfers between devices with their start and end apart: 3 -> 0, of which waited for: 3 -> 0; matrix products, arithmetic and copies ran while one was open for 0% -> 0% of each run, Pallas kernels for 0% -> 0%
where the time goes in v1:
time: 291 us; the launch traced here: 290 us
  Pallas kernels  254 us (87%)
  matrix products  14.2 us (5%)
  other arithmetic  12.9 us (4%)
  between operations  5.98 us (2%)
    pallas_call x1, Pallas kernels, gram_sums(): pl.pallas_call(gram_kernel, out_shape=(jax.ShapeDtypeStruct((ROWS, cells)...  192 us
    pallas_call x1, Pallas kernels, inverse_factor(): pl.pallas_call(inverse_factor_kernel, out_shape=jax.ShapeDtypeStruct((n,...  61.8 us
    dot_general x1, matrix products, local(): upper_second = jnp.dot(scaled[B:], gram, precision=lax.Precision.HIGH)  7.38 us

profile of v1, /device:TPU:0, one launch (start us, length us, event | category | flops | bytes accessed | tf_op | source)
XLA Modules:
  0.0 289.7 jit_solution(15747077154011585311)
XLA Ops:
  0.6 1.3 fusion.13
  7.2 0.7 fusion.8
  7.9 2.4 dynamic-slice_select_fusion.1
  10.3 1.9 pad_maximum_fusion.1.cand_ref
  12.1 192.0 %shard_map.41 = (bf16[1024,1536]{1,0:T(8,128)(2,1)}, f32[1024,2048]{1,0:T(8,128)}, f32[1024,1024]{1,0:T(8,128)}) custom-call(bf16[1024,1536]{1,0:T(8,128)(2,1)} %pad_maximum_fusion.1.cand_ref, bf16[2048,1536]{1,0:T(8,128)(2,1)} %orb_ref.1), custom_call_target="tpu_custom_call" | custom-call | tf_op jit(solution)/shard_map/pallas_call | solution.py:327
  204.2 3.1 %broadcast_multiply_fusion.1.g_ref = f32[1024,1024]{1,0:T(8,128)S(1)} fusion(f32[1024,1024]{1,0:T(8,128)} %get-tuple-element.5), kind=kLoop, calls=%fused_computation.8 | loop fusion | flops 1048576 | bytes 8388608 | tf_op jit(solution)/shard_map/mul | solution.py:371
  207.3 0.0 copy-start
  207.3 61.8 %shard_map.42 = f32[1024,1024]{1,0:T(8,128)S(1)} custom-call(f32[1024,1024]{1,0:T(8,128)S(1)} %broadcast_multiply_fusion.1.g_ref), custom_call_target="tpu_custom_call" | custom-call | tf_op jit(solution)/shard_map/pallas_call | solution.py:102
  269.1 0.0 copy-done
  269.1 1.0 fusion.6
  270.1 0.0 slice-start
  270.1 2.1 convolution_add_fusion
  272.2 0.0 slice-start.1
  272.2 0.9 broadcast_multiply_fusion
  273.1 0.0 slice-done
  273.1 1.4 slice-done.1
  274.6 7.4 %convolution_select_fusion = f32[512,2048]{1,0:T(8,128)S(1)} fusion(f32[1024,2048]{1,0:T(8,128)S(1)} %bitcast.6, f32[1024,1024]{1,0:T(8,128)S(1)} %broadcast_multiply_fusion, pred[2048]{0:T(1024)(128)(4,1)S(1)} %fusion.8), kind=kOutput, calls=%fused_computation.4 | convolution fusion | flops 6443499520 | bytes 14682112 | tf_op jit(solution)/shard_map/dot_general | solution.py:375
  281.9 3.8 %fusion = f32[512,2048]{1,0:T(8,128)S(1)} fusion(f32[1024,2048]{1,0:T(8,128)S(1)} %bitcast.6, f32[1024,1024]{1,0:T(8,128)S(1)} %broadcast_multiply_fusion), kind=kOutput, calls=%fused_computation.1 | convolution fusion | flops 3221225472 | bytes 9437184 | tf_op jit(solution)/shard_map/dot_general | solution.py:374
  285.7 4.0 %pad_maximum_fusion = f32[1024,2048]{1,0:T(8,128)} fusion(f32[512,2048]{1,0:T(8,128)S(1)} %convolution_select_fusion, f32[512,2048]{1,0:T(8,128)S(1)} %fusion), kind=kLoop, calls=%fused_computation | loop fusion | flops 2097152 | bytes 16777216 | tf_op jit(solution)/shard_map/concatenate | solution.py:377
  (1 shorter events, 0.0 us)
Async XLA Ops:
  207.3 61.8 %copy-start = (bf16[1024,1536]{1,0:T(8,128)(2,1)S(1)}, bf16[1024,1536]{1,0:T(8,128)(2,1)}, u32[]{:S(2)}) copy-start(bf16[1024,1536]{1,0:T(8,128)(2,1)} %get-tuple-element.7) | copy-start | bytes 9437188
  270.1 3.1 %slice-start = ((s8[8388608]{0:T(1024)(128)(4,1)}), s8[4194304]{0:T(1024)(128)(4,1)S(1)}, s32[]{:S(2)}) async-start(s8[8388608]{0:T(1024)(128)(4,1)} %bitcast.5), calls=%async_computation | async-start | bytes 8388608
  272.2 2.3 slice-start.1

commit v2 on v0

v2 whole, which is shorter than its diff:
```python
import jax
import jax.numpy as jnp
from jax import lax
from jax.experimental import pallas as pl
from jax.experimental.pallas import tpu as pltpu
from jax.sharding import PartitionSpec as P

B = 512
BPD = 4
BLK = 128
SUB = 8
HI = lax.Precision.HIGHEST


def invert_block(block_ref, out_ref, hook):
    shape = (SUB, BLK)
    lane = lax.broadcasted_iota(jnp.int32, shape, 1)
    row = lax.broadcasted_iota(jnp.int32, shape, 0)
    count = BLK // SUB
    tiles = [block_ref[SUB * i : SUB * i + SUB, :] for i in range(count)]
    for c in range(count):
        hook(c)
        low = SUB * c
        here = jnp.logical_and(lane >= low, lane < low + SUB)
        pivot = tiles[c]
        column = [jnp.broadcast_to(pivot[:, low + m : low + m + 1], shape) for m in range(SUB)]
        a = {}
        for m in range(SUB):
            for i in range(m, SUB):
                a[i, m] = jnp.broadcast_to(column[m][i : i + 1, :], shape)
        marked = jnp.where(here, (lane - low == row).astype(jnp.float32), pivot)
        y = [jnp.broadcast_to(marked[k : k + 1, :], shape) for k in range(SUB)]
        t = {}
        for m in range(SUB):
            r = lax.rsqrt(a[m, m])
            for i in range(m + 1, SUB):
                a[i, m] = a[i, m] * r
            y[m] = y[m] * r
            for k in range(m):
                t[m, k] = t[m, k] * r
            t[m, m] = r
            for j in range(m + 1, SUB):
                for i in range(j, SUB):
                    a[i, j] = a[i, j] - a[i, m] * a[j, m]
            for i in range(m + 1, SUB):
                y[i] = y[i] - a[i, m] * y[m]
                for k in range(m):
                    t[i, k] = t[i, k] - a[i, m] * t[m, k]
                t[i, m] = -(a[i, m] * r)
        tile = y[0]
        for i in range(1, SUB):
            tile = jnp.where(row == i, y[i], tile)
        out_ref[low : low + SUB, :] = jnp.where(lane < low + SUB, tile, 0.0)
        if c == count - 1:
            break
        z = []
        for k in range(SUB):
            acc = t[k, k] * y[k]
            for i in range(k + 1, SUB):
                acc = acc + t[i, k] * y[i]
            z.append(acc)
        for r in range(c + 1, count):
            terms = [jnp.broadcast_to(tiles[r][:, low + m : low + m + 1], shape) * z[m] for m in range(SUB)]
            while len(terms) > 1:
                terms = [terms[i] + terms[i + 1] for i in range(0, len(terms), 2)]
            tiles[r] = jnp.where(here, 0.0, tiles[r]) - terms[0]


ROWS = 2 * B
LOCAL = 2048
WIDE = 1024
RING = 4
PIECES = 2
PIECE = B // 2 // PIECES
CELLS = 49152
MESH = pl.DeviceIdType.MESH
UNIT_SHAPES = ((256, 256), (512, 256), (512, 1024), (512, 1024))
COPIES = 22


def remote(src, dst, send, recv, axis, other):
    return pltpu.make_async_remote_copy(
        src_ref=src, dst_ref=dst, send_sem=send, recv_sem=recv, device_id={axis: other}, device_id_type=MESH)


class HalfReduce:
    def __init__(self, data, first, second, third, send, recv, free, p, p_next, p_prev, q, q_next, q_prev, y, y_mate):
        self.data, self.first, self.second, self.third, self.free = data, first, second, third, free
        self.p_ring, self.q_ring = (p_next, p_prev), (q_next, q_prev)
        size = data.shape[0]
        one, two, three = size // 4, size // 16, size // 32
        base = p * one
        low = base + q * two
        count = iter(range(COPIES))

        def make(src, dst, other):
            i = next(count)
            return remote(src, dst, send.at[i], recv.at[i], "grid", other)

        def cut(start, pos, length):
            half = length // 2
            return lambda turn, which: pl.ds(
                pl.multiple_of(start + ((pos + turn) % RING) * length + which * half, 8), half)

        def reduce_copies(rows, slots, following, previous):
            return [
                make(data.at[rows[2, 0]], slots.at[0], following),
                make(data.at[rows[2, 1]], slots.at[1], previous),
                make(data.at[rows[1, 1]], slots.at[2], following),
                make(data.at[rows[3, 0]], slots.at[3], previous),
                make(slots.at[0], slots.at[4], following),
                make(slots.at[1], slots.at[5], previous),
            ]

        def gather_copies(rows, own, following, previous):
            return [
                make(data.at[own], data.at[own], following),
                make(data.at[own], data.at[own], previous),
                make(data.at[rows[3, 0]], data.at[rows[3, 0]], following),
                make(data.at[rows[1, 1]], data.at[rows[1, 1]], previous),
            ]

        cut_p, cut_q = cut(0, p, one), cut(base, q, two)
        self.rows_p = {(t, w): cut_p(t, w) for t in range(RING) for w in range(2)}
        self.rows_q = {(t, w): cut_q(t, w) for t in range(RING) for w in range(2)}
        own_p = pl.ds(pl.multiple_of(base, 8), one)
        own_q = pl.ds(pl.multiple_of(low, 8), two)
        self.own_y = pl.ds(pl.multiple_of(low + y * three, 8), three)
        self.rest_y = pl.ds(pl.multiple_of(low + (1 - y) * three, 8), three)
        self.reduce_p = reduce_copies(self.rows_p, first, p_next, p_prev)
        self.reduce_q = reduce_copies(self.rows_q, second, q_next, q_prev)
        self.swap = make(data.at[self.rest_y], third.at[0], y_mate)
        self.share = make(data.at[self.own_y], third.at[1], y_mate)
        self.gather_q = gather_copies(self.rows_q, own_q, q_next, q_prev)
        self.gather_p = gather_copies(self.rows_p, own_p, p_next, p_prev)

    def begin(self, copies):
        for copy in copies[:4]:
            copy.start()

    def middle(self, copies, rows, slots):
        copies[0].wait_recv()
        slots[0] = slots[0] + self.data[rows[1, 0], :]
        copies[4].start()
        copies[1].wait_recv()
        slots[1] = slots[1] + self.data[rows[3, 1], :]
        copies[5].start()

    def end(self, copies, rows, slots, ring, free):
        copies[2].wait_recv()
        copies[3].wait_recv()
        copies[4].wait_recv()
        self.data[rows[0, 0], :] = self.data[rows[0, 0], :] + (slots[3] + slots[4])
        copies[5].wait_recv()
        self.data[rows[0, 1], :] = self.data[rows[0, 1], :] + (slots[2] + slots[5])
        for copy in copies:
            copy.wait_send()
        for other in ring:
            pl.semaphore_signal(free, inc=1, device_id={"grid": other}, device_id_type=MESH)

    def spread(self, copies, free):
        pl.semaphore_wait(free, 2)
        copies[0].start()
        copies[1].start()

    def forward(self, copies):
        copies[0].wait_recv()
        copies[2].start()
        copies[1].wait_recv()
        copies[3].start()

    def settle(self, copies):
        copies[2].wait_recv()
        copies[3].wait_recv()
        for copy in copies:
            copy.wait_send()

    def step(self, i):
        p, q = self.reduce_p, self.reduce_q
        if i == 0:
            self.begin(p)
        elif i == 1:
            self.middle(p, self.rows_p, self.first)
        elif i == 2:
            self.end(p, self.rows_p, self.first, self.p_ring, self.free.at[0])
            self.begin(q)
        elif i == 3:
            self.middle(q, self.rows_q, self.second)
        elif i == 4:
            self.end(q, self.rows_q, self.second, self.q_ring, self.free.at[1])
            self.swap.start()
        elif i == 5:
            self.swap.wait_recv()
            self.data[self.own_y, :] = self.data[self.own_y, :] + self.third[0]
            self.share.start()
        elif i == 6:
            self.share.wait_recv()
            self.swap.wait_send()
            self.share.wait_send()
            self.data[self.rest_y, :] = self.third[1]
            self.spread(self.gather_q, self.free.at[1])
        elif i == 7:
            self.forward(self.gather_q)
        elif i == 8:
            self.settle(self.gather_q)
            self.spread(self.gather_p, self.free.at[0])
        elif i == 9:
            self.forward(self.gather_p)
        elif i == 10:
            self.settle(self.gather_p)


STEPS = 11


def whole_kernel(cand_ref, orb_ref, panel_out, gram_out, mixing_out,
                 panel, merged, from_core, from_chip, tiles_a, tiles_b, main, mate_a, mate_b,
                 s00, s01, s02, s10, s11, s12, s20, s21, s22, s30, s31, s32,
                 work, block, inv, coupling, mixing,
                 panel_send, panel_recv, send, recv, free, local_sem):
    o = lax.axis_index("orb")
    g = lax.axis_index("grid")
    core = o % 2
    mate = o + 1 - 2 * core
    across = (o + 2) % 4
    x = g // 8
    y = (g // 4) % 2
    z = g % 4
    x_next = ((x + 1) % RING) * 8 + y * 4 + z
    x_prev = ((x + 3) % RING) * 8 + y * 4 + z
    z_next = x * 8 + y * 4 + (z + 1) % RING
    z_prev = x * 8 + y * 4 + (z + 3) % RING
    y_mate = x * 8 + (1 - y) * 4 + z

    barrier = pltpu.get_barrier_semaphore()
    for other in (mate, across):
        pl.semaphore_signal(barrier, inc=1, device_id={"orb": other}, device_id_type=MESH)
    for other in (x_next, x_prev, z_next, z_prev, y_mate):
        pl.semaphore_signal(barrier, inc=1, device_id={"grid": other}, device_id_type=MESH)
    pl.semaphore_wait(barrier, 7)

    data = ([tiles_a.at[0], tiles_a.at[1]], [tiles_b.at[0], tiles_b.at[1]],
            [main.at[0, 0], main.at[0, 1]], [main.at[1, 0], main.at[1, 1]])
    slots = ((s00, s01, s02), (s10, s11, s12), (s20, s21, s22), (s30, s31, s32))
    units = []
    for u in range(4):
        first, second, third = slots[u]
        units.append([
            HalfReduce(data[u][0], first.at[0], second.at[0], third.at[0], send.at[u, 0], recv.at[u, 0],
                       free.at[u, 0], x, x_next, x_prev, z, z_next, z_prev, y, y_mate),
            HalfReduce(data[u][1], first.at[1], second.at[1], third.at[1], send.at[u, 1], recv.at[u, 1],
                       free.at[u, 1], z, z_next, z_prev, x, x_next, x_prev, y, y_mate),
        ])
    done = [0] * 4

    def advance(u, upto=None):
        upto = done[u] + 1 if upto is None else upto
        while done[u] < upto:
            for half in units[u]:
                half.step(done[u])
            done[u] += 1

    quarter = B // 2

    def part(t, which, j):
        return pl.ds(pl.multiple_of(t * B + which * quarter + j * PIECE, PIECE), PIECE)

    def orb_copy(src, dst, other, i):
        return remote(src, dst, panel_send.at[i], panel_recv.at[i], "orb", other)

    pieces = [(t, j) for t in range(2) for j in range(PIECES)]
    mine = {tj: part(tj[0], core, tj[1]) for tj in pieces}
    theirs = {tj: part(tj[0], 1 - core, tj[1]) for tj in pieces}
    n = len(pieces)
    give = {tj: orb_copy(cand_ref.at[theirs[tj]], from_core.at[i], mate, i) for i, tj in enumerate(pieces)}
    cross = {tj: orb_copy(merged.at[i], from_chip.at[i], across, n + i) for i, tj in enumerate(pieces)}
    share = {tj: orb_copy(panel.at[mine[tj]], panel.at[mine[tj]], mate, 2 * n + i) for i, tj in enumerate(pieces)}
    for tj in pieces:
        give[tj].start()
    for i, tj in enumerate(pieces):
        give[tj].wait_recv()
        merged[i] = cand_ref[mine[tj], :] + from_core[i]
        cross[tj].start()

    def collect(t):
        for j in range(PIECES):
            i = pieces.index((t, j))
            cross[t, j].wait_recv()
            panel[mine[t, j], :] = merged[i] + from_chip[i]
            share[t, j].start()

    def receive(t):
        for j in range(PIECES):
            share[t, j].wait_recv()

    contract = (((1,), (1,)), ((), ()))

    def product(rows, columns):
        return lax.dot_general(rows, columns, contract, preferred_element_type=jnp.float32)

    def core_rows(t):
        return panel[pl.ds(pl.multiple_of(t * B + core * quarter, quarter), quarter), :]

    def main_gram(t):
        for h in range(2):
            def column(i, carry, h=h):
                at = pl.multiple_of(i * 256, 256)
                main[t, h, :, pl.ds(at, 256)] = product(
                    panel[t * B : (t + 1) * B, :], orb_ref[pl.ds(h * WIDE + at, 256), :])
                return carry

            lax.fori_loop(0, WIDE // 256, column, 0)

    collect(0)
    receive(0)
    for h in range(2):
        tiles_a[h] = product(core_rows(0), panel[h * quarter : (h + 1) * quarter, :])
    advance(0)
    main_gram(0)
    advance(0)
    advance(2)
    collect(1)
    advance(0)
    advance(0)
    receive(1)
    advance(0)
    for h in range(2):
        columns = panel[B + h * quarter : B + (h + 1) * quarter, :]
        tiles_b[h, :quarter, :] = product(core_rows(0), columns)
        tiles_b[h, quarter:, :] = product(core_rows(1), columns)
    advance(0)
    advance(1)
    advance(0)
    main_gram(1)
    advance(0)
    advance(0)
    advance(0)
    advance(0)
    advance(2)
    save_panel = pltpu.make_async_copy(panel, panel_out, local_sem.at[0])
    save_panel.start()

    share_a = [orb_copy(tiles_a.at[h], mate_a.at[h], mate, 3 * n + h) for h in range(2)]
    share_b = [orb_copy(tiles_b.at[h], mate_b.at[h], mate, 3 * n + 2 + h) for h in range(2)]
    scale = 1.0 / CELLS
    own_rows = pl.ds(pl.multiple_of(core * quarter, quarter), quarter)
    mate_rows = pl.ds(pl.multiple_of((1 - core) * quarter, quarter), quarter)
    for copy in share_a:
        copy.start()
    for h in range(2):
        columns = slice(h * quarter, (h + 1) * quarter)
        work[own_rows, columns] = tiles_a[h] * scale
        share_a[h].wait_recv()
        work[mate_rows, columns] = mate_a[h] * scale

    def factor(phase, hooks):
        column = lax.broadcasted_iota(jnp.int32, (BLK, B), 1)
        low = phase * B

        def step(k, carry):
            start = pl.multiple_of(k * BLK, BLK)
            here = pl.ds(start, BLK)
            block[...] = work[here, here]

            def hook(c):
                for i in range(B // BLK):
                    if (i, c) in hooks:
                        pl.when(k == i)(hooks[i, c])

            invert_block(block, inv, hook)
            t = inv[...]
            row = jnp.dot(t, work[here, :], precision=HI, preferred_element_type=jnp.float32)
            mixing[pl.ds(low + start, BLK), low : low + B] = jnp.where(column < start, row, 0.0)
            mixing[pl.ds(low + start, BLK), pl.ds(low + start, BLK)] = t
            work[here, :] = row
            work[here, here] = t

            def update(i, carry):
                rows = pl.ds(pl.multiple_of(i * BLK, BLK), BLK)
                u = work[here, rows]
                work[rows, here] = jnp.zeros((BLK, BLK), jnp.float32)
                work[rows, :] -= lax.dot_general(
                    u, work[here, :], (((0,), (0,)), ((), ())), precision=HI, preferred_element_type=jnp.float32)
                return carry

            return lax.fori_loop(k + 1, B // BLK, update, carry)

        lax.fori_loop(0, B // BLK, step, 0)

    def schedule(order):
        hooks = {}
        spots = [(k, c) for k in range(B // BLK) for c in (0, 4, 8, 12)]
        for spot, names in zip(spots, order):
            todo = []
            for u in names:
                if done[u] < STEPS:
                    todo += [(half, done[u]) for half in units[u]]
                    done[u] += 1
            if todo:
                hooks[spot] = lambda todo=todo: [half.step(i) for half, i in todo] and None
        return hooks

    factor(0, schedule(ORDER_A))
    for copy in share_b:
        copy.start()
    for h in range(2):
        columns = slice(h * quarter, (h + 1) * quarter)
        coupling[own_rows, columns] = tiles_b[h, :quarter, :] * scale
        work[own_rows, columns] = tiles_b[h, quarter:, :] * scale
        share_b[h].wait_recv()
        coupling[mate_rows, columns] = mate_b[h, :quarter, :] * scale
        work[mate_rows, columns] = mate_b[h, quarter:, :] * scale
    mixing[:B, B:] = jnp.zeros((B, B), jnp.float32)
    first = mixing[:B, :B]
    coupling[...] = jnp.dot(first, coupling[...], precision=HI, preferred_element_type=jnp.float32)
    turned = (((0,), (0,)), ((), ()))
    work[...] -= lax.dot_general(
        coupling[...], coupling[...], turned, precision=HI, preferred_element_type=jnp.float32)
    coupling[...] = lax.dot_general(
        coupling[...], mixing[:B, :B], turned, precision=HI, preferred_element_type=jnp.float32)
    factor(1, schedule(ORDER_B))
    mixing[B:, :B] = -jnp.dot(mixing[B:, B:], coupling[...], precision=HI, preferred_element_type=jnp.float32)
    save_mixing = pltpu.make_async_copy(mixing, mixing_out, local_sem.at[1])
    save_mixing.start()
    saves = [save_panel, save_mixing]
    while done[2] < STEPS or done[3] < STEPS:
        for u in (2, 3):
            if done[u] < STEPS:
                advance(u)
    for t in range(2):
        for h in range(2):
            saves.append(pltpu.make_async_copy(
                main.at[t, h], gram_out.at[pl.ds(t * B, B), pl.ds(h * WIDE, WIDE)], local_sem.at[2 + 2 * t + h]))
            saves[-1].start()
    for copy in [*give.values(), *cross.values(), *share.values(), *share_a, *share_b]:
        copy.wait_send()
    for save in saves:
        save.wait()


ORDER_A = [(1,), (1,), (2,), (3,), (1,), (1,), (2,), (3,), (1,), (1,), (2,), (1,), (3,), (1,), (1,), (1,)]
ORDER_B = [(2,), (3,), (2,), (3,), (2,), (3,), (2,), (3,), (2,), (3,), (2,), (3,), (2,), (3,), (2,), (3,)]


def whole(cand, orbitals):
    cells = orbitals.shape[1]
    f32 = jnp.float32
    bf16 = jnp.bfloat16
    any_space = pl.BlockSpec(memory_space=pl.ANY)
    n = 2 * PIECES
    slots = []
    for rows, columns in UNIT_SHAPES:
        slots += [
            pltpu.VMEM((2, 6, rows // 8, columns), f32),
            pltpu.VMEM((2, 6, rows // 32, columns), f32),
            pltpu.VMEM((2, 2, rows // 32, columns), f32),
        ]
    return pl.pallas_call(
        whole_kernel,
        out_shape=(
            jax.ShapeDtypeStruct((ROWS, cells), bf16),
            jax.ShapeDtypeStruct((ROWS, LOCAL), f32),
            jax.ShapeDtypeStruct((ROWS, ROWS), f32),
        ),
        in_specs=[pl.BlockSpec(memory_space=pltpu.VMEM)] * 2,
        out_specs=(any_space,) * 3,
        scratch_shapes=[
            pltpu.VMEM((ROWS, cells), bf16),
            pltpu.VMEM((n, PIECE, cells), bf16),
            pltpu.VMEM((n, PIECE, cells), bf16),
            pltpu.VMEM((n, PIECE, cells), bf16),
            pltpu.VMEM((2, 256, 256), f32),
            pltpu.VMEM((2, 512, 256), f32),
            pltpu.VMEM((2, 2, B, WIDE), f32),
            pltpu.VMEM((2, 256, 256), f32),
            pltpu.VMEM((2, 512, 256), f32),
            *slots,
            pltpu.VMEM((B, B), f32),
            pltpu.VMEM((BLK, BLK), f32),
            pltpu.VMEM((BLK, BLK), f32),
            pltpu.VMEM((B, B), f32),
            pltpu.VMEM((ROWS, ROWS), f32),
            pltpu.SemaphoreType.DMA((3 * n + 4,)),
            pltpu.SemaphoreType.DMA((3 * n + 4,)),
            pltpu.SemaphoreType.DMA((4, 2, COPIES)),
            pltpu.SemaphoreType.DMA((4, 2, COPIES)),
            pltpu.SemaphoreType.REGULAR((4, 2, 2)),
            pltpu.SemaphoreType.DMA((6,)),
        ],
        compiler_params=pltpu.CompilerParams(
            collective_id=0, has_side_effects=True, vmem_limit_bytes=60 << 20),
    )(cand, orbitals)


def local(orbitals, block_order):
    own_index = lax.axis_index("orb")
    local_cols = orbitals.shape[0]
    first_block = block_order[0]
    second_block = block_order[1]

    def candidate(block_index):
        piece = lax.dynamic_slice_in_dim(orbitals, block_index % BPD * B, B, 0)
        return jnp.where(block_index // BPD == own_index, piece, 0).astype(piece.dtype)

    cand = jnp.concatenate([candidate(first_block), candidate(second_block)], 0)
    panel, gram, mixing = whole(cand, orbitals)
    scale = jnp.float32(1.0 / CELLS)
    column_blocks = (own_index * local_cols + jnp.arange(local_cols, dtype=jnp.int32)) // B
    scaled = mixing * scale
    upper_first = jnp.dot(scaled[:B, :B], gram[:B], precision=lax.Precision.HIGH)
    upper_second = jnp.dot(scaled[B:], gram, precision=lax.Precision.HIGH)
    upper_second = jnp.where((column_blocks == first_block)[None, :], jnp.float32(0.0), upper_second)
    factor_rows = jnp.concatenate([upper_first, upper_second], 0)
    rows_dev = ROWS // lax.axis_size("orb")
    mixing_rows = lax.dynamic_slice_in_dim(mixing, own_index * rows_dev, rows_dev, 0)
    high = lax.reduce_precision(mixing_rows, 8, 7)
    low = (mixing_rows - high).astype(jnp.bfloat16)
    ortho = jnp.dot(high.astype(jnp.bfloat16), panel, preferred_element_type=jnp.float32) + jnp.dot(
        low, panel, preferred_element_type=jnp.float32)
    return (factor_rows, ortho)


def solution(mesh):
    return jax.shard_map(
        local,
        mesh=mesh,
        in_specs=(P("orb", "grid"), P()),
        out_specs=(P(None, "orb"), P("orb", "grid")),
        check_vma=False,
    )
```

time: 949 us -> 240 us (0.25)
  waiting for transfers between devices: 555 us -> 0 us
  other arithmetic: 263 us -> 9.41 us
  Pallas kernels: 0 us -> 203 us
  matrix products: 67 us -> 18.3 us
  local copies, waits for them, and re-layouts: 34.7 us -> 3.01 us
  between operations: 25 us -> 5.97 us
    psum x3 -> x0, waiting for transfers between devices: 554 us -> none  [the longest x1 386 us: local(): summed = lax.psum(local_gram, 'grid')]
    another operation x35 -> x0, other arithmetic: 243 us -> none  [the longest x15 81.3 us: factor_pieces(): second_chol = jnp.linalg.cholesky(schur_block)]
    pallas_call x0 -> x1, Pallas kernels: none -> 203 us  [whole(): pl.pallas_call(whole_kernel, out_shape=(jax.ShapeDtypeStruct((ROWS, cells...]
    dot_general x9 -> x4, matrix products: 48.2 us -> 18.3 us  [the longest x1 7.37 us: local(): upper_second = jnp.dot(scaled[B:], gram, precision=lax.Precision.HIGH)]
    another operation x35 -> x0, local copies, waits for them, and re-layouts: 20.9 us -> none  [the longest x12 11.3 us: factor_pieces(): jax.scipy.linalg.solve_triangular(second_chol, identity, lower=True)]
    another operation x26 -> x0, matrix products: 18.8 us -> none  [the longest x6 7.92 us: factor_pieces(): second_chol = jnp.linalg.cholesky(schur_block)]
  transfers between devices with their start and end apart: 3 -> 0, of which waited for: 3 -> 0; matrix products, arithmetic and copies ran while one was open for 0% -> 0% of each run, Pallas kernels for 0% -> 0%
where the time goes in v2:
time: 240 us; the launch traced here: 239 us
  Pallas kernels  203 us (85%)
  matrix products  18.3 us (8%)
  other arithmetic  9.41 us (4%)
  between operations  5.97 us (2%)
  local copies, waits for them, and re-layouts  3.01 us (1%)
    pallas_call x1, Pallas kernels, whole(): pl.pallas_call(whole_kernel, out_shape=(jax.ShapeDtypeStruct((ROWS, cells...  203 us
    dot_general x1, matrix products, local(): upper_second = jnp.dot(scaled[B:], gram, precision=lax.Precision.HIGH)  7.37 us

profile of v2, /device:TPU:0, one launch (start us, length us, event | category | flops | bytes accessed | tf_op | source)
XLA Modules:
  0.0 239.4 jit_solution(14347747505610016049)
XLA Ops:
  0.6 1.3 fusion.13
  7.2 0.7 fusion.8
  7.9 2.4 %dynamic-slice_select_fusion.1 = (bf16[512,1536]{1,0:T(8,128)(2,1)S(1)}, bf16[512,1536]{1,0:T(8,128)(2,1)S(1)}) fusion(bf16[2048,1536]{1,0:T(8,128)(2,1)} %orb_ref.1, s32[]{:T(128)S(6)} %select_n.57, pred[]{:T(512)S(6)} %eq.19, s32[]{:T(128)S(6)} %select_n.62, pred[]{:T(512)S(6)} %eq.20), kind=kLoop, calls=%fused_computation.9 | loop fusion | flops 1572864 | bytes 6291466 | tf_op jit(solution)/shard_map/jit(_where)/select_n | solution.py:503
  10.3 1.9 pad_maximum_fusion.1.cand_ref
  12.1 202.7 %shard_map.41 = (bf16[1024,1536]{1,0:T(8,128)(2,1)}, f32[1024,2048]{1,0:T(8,128)}, f32[1024,1024]{1,0:T(8,128)}) custom-call(bf16[1024,1536]{1,0:T(8,128)(2,1)} %pad_maximum_fusion.1.cand_ref, bf16[2048,1536]{1,0:T(8,128)(2,1)} %orb_ref.1), custom_call_target="tpu_custom_call" | custom-call | tf_op jit(solution)/shard_map/pallas_call | solution.py:458
  214.9 0.0 copy-start
  214.9 0.0 copy-start.1
  214.9 3.3 %fusion.6 = f32[256,1536]{1,0:T(8,128)S(1)} fusion(bf16[1024,1536]{1,0:T(8,128)(2,1)} %get-tuple-element.7, f32[1024,1024]{1,0:T(8,128)} %get-tuple-element.5, s32[]{:T(128)S(6)} %select_n.66), kind=kOutput, calls=%fused_computation.14 | convolution fusion | flops 805830656 | bytes 5767172 | tf_op jit(solution)/shard_map/dot_general | solution.py:518
  218.2 0.0 copy-done
  218.3 0.0 slice-start
  218.3 3.5 %convolution_add_fusion = f32[256,1536]{1,0:T(8,128)} fusion(f32[256,1536]{1,0:T(8,128)S(1)} %fusion.6, bf16[1024,1536]{1,0:T(8,128)(2,1)S(1)} %copy-done, f32[1024,1024]{1,0:T(8,128)} %get-tuple-element.5, s32[]{:T(128)S(6)} %select_n.66), kind=kOutput, calls=%fused_computation.5 | convolution fusion | flops 806486016 | bytes 7340036 | tf_op jit(solution)/shard_map/dot_general | solution.py:518
  221.8 0.0 copy-done.1
  221.8 0.0 slice-start.1
  221.8 0.5 broadcast_multiply_fusion
  222.3 0.0 slice-done
  222.3 1.7 slice-done.1
  224.0 7.4 %convolution_select_fusion = f32[512,2048]{1,0:T(8,128)S(1)} fusion(f32[1024,2048]{1,0:T(8,128)S(1)} %bitcast.6, f32[1024,1024]{1,0:T(8,128)S(1)} %broadcast_multiply_fusion, pred[2048]{0:T(1024)(128)(4,1)S(1)} %fusion.8), kind=kOutput, calls=%fused_computation.4 | convolution fusion | flops 6443499520 | bytes 14682112 | tf_op jit(solution)/shard_map/dot_general | solution.py:511
  231.4 4.0 %fusion = f32[512,2048]{1,0:T(8,128)S(1)} fusion(f32[1024,2048]{1,0:T(8,128)S(1)} %bitcast.6, f32[1024,1024]{1,0:T(8,128)S(1)} %broadcast_multiply_fusion), kind=kOutput, calls=%fused_computation.1 | convolution fusion | flops 3221225472 | bytes 9437184 | tf_op jit(solution)/shard_map/dot_general | solution.py:510
  235.4 4.0 %pad_maximum_fusion = f32[1024,2048]{1,0:T(8,128)} fusion(f32[512,2048]{1,0:T(8,128)S(1)} %convolution_select_fusion, f32[512,2048]{1,0:T(8,128)S(1)} %fusion), kind=kLoop, calls=%fused_computation | loop fusion | flops 2097152 | bytes 16777216 | tf_op jit(solution)/shard_map/concatenate | solution.py:513
  (1 shorter events, 0.0 us)
Async XLA Ops:
  214.9 3.4 %copy-start = (bf16[1024,1536]{1,0:T(8,128)(2,1)S(1)}, bf16[1024,1536]{1,0:T(8,128)(2,1)}, u32[]{:S(2)}) copy-start(bf16[1024,1536]{1,0:T(8,128)(2,1)} %get-tuple-element.7) | copy-start | bytes 9437188
  214.9 6.9 %copy-start.1 = (f32[1024,1024]{1,0:T(8,128)S(1)}, f32[1024,1024]{1,0:T(8,128)}, u32[]{:S(2)}) copy-start(f32[1024,1024]{1,0:T(8,128)} %get-tuple-element.5) | copy-start | bytes 12582916
  218.3 4.0 %slice-start = ((s8[8388608]{0:T(1024)(128)(4,1)}), s8[4194304]{0:T(1024)(128)(4,1)S(1)}, s32[]{:S(2)}) async-start(s8[8388608]{0:T(1024)(128)(4,1)} %bitcast.5), calls=%async_computation | async-start | bytes 8388608
  221.8 2.2 slice-start.1

commit v3 on v2

--- a/solution.py
+++ b/solution.py
@@ -74,8 +74,9 @@
 PIECE = B // 2 // PIECES
 CELLS = 49152
 MESH = pl.DeviceIdType.MESH
-UNIT_SHAPES = ((256, 256), (512, 256), (512, 1024), (512, 1024))
-COPIES = 22
+UNIT_SHAPES = ((256, 256), (512, 256)) + ((256, 1024),) * 4
+COPIES = 24
+PEERS = [(turn, flip) for turn in range(RING) for flip in range(2)][1:]
 
 
 def remote(src, dst, send, recv, axis, other):
@@ -83,8 +84,11 @@
         src_ref=src, dst_ref=dst, send_sem=send, recv_sem=recv, device_id={axis: other}, device_id_type=MESH)
 
 
-class HalfReduce:
-    def __init__(self, data, first, second, third, send, recv, free, p, p_next, p_prev, q, q_next, q_prev, y, y_mate):
+class RingReduce:
+    steps = 11
+
+    def __init__(self, data, first, second, third, send, recv, free, p, p_next, p_prev, q, q_next, q_prev, y, device):
+        y_mate = device(q, 1 - y)
         self.data, self.first, self.second, self.third, self.free = data, first, second, third, free
         self.p_ring, self.q_ring = (p_next, p_prev), (q_next, q_prev)
         size = data.shape[0]
@@ -210,14 +214,89 @@
             self.settle(self.gather_p)
 
 
-STEPS = 11
+class DirectReduce(RingReduce):
+    steps = 7
+
+    def __init__(self, data, first, second, third, send, recv, free, p, p_next, p_prev, q, q_next, q_prev, y, device):
+        self.data, self.first, self.second, self.free = data, first, second, free
+        self.p_ring = (p_next, p_prev)
+        size = data.shape[0]
+        one, three = size // 4, size // 32
+        half = one // 2
+        base = p * one
+        count = iter(range(COPIES))
+
+        def make(src, dst, other):
+            i = next(count)
+            return remote(src, dst, send.at[i], recv.at[i], "grid", other)
+
+        def rows(turn, which):
+            return pl.ds(pl.multiple_of(((p + turn) % RING) * one + which * half, 8), half)
+
+        def member(turn, flip):
+            return pl.ds(pl.multiple_of(base + (((q + turn) % RING) * 2 + (y + flip) % 2) * three, 8), three)
+
+        self.rows_p = {(t, w): rows(t, w) for t in range(RING) for w in range(2)}
+        self.own = member(0, 0)
+        self.origin = [member(RING - turn, flip) for turn, flip in PEERS]
+        own_p = pl.ds(pl.multiple_of(base, 8), one)
+        others = [device((q + turn) % RING, (y + flip) % 2) for turn, flip in PEERS]
+        r = self.rows_p
+        self.reduce_p = [
+            make(data.at[r[2, 0]], first.at[0], p_next),
+            make(data.at[r[2, 1]], first.at[1], p_prev),
+            make(data.at[r[1, 1]], first.at[2], p_next),
+            make(data.at[r[3, 0]], first.at[3], p_prev),
+            make(first.at[0], first.at[4], p_next),
+            make(first.at[1], first.at[5], p_prev),
+        ]
+        self.scatter = [make(data.at[member(*peer)], second.at[i], others[i]) for i, peer in enumerate(PEERS)]
+        self.share = [make(data.at[self.own], second.at[7 + i], others[i]) for i in range(7)]
+        self.gather_p = [
+            make(data.at[own_p], data.at[own_p], p_next),
+            make(data.at[own_p], data.at[own_p], p_prev),
+            make(data.at[r[3, 0]], data.at[r[3, 0]], p_next),
+            make(data.at[r[1, 1]], data.at[r[1, 1]], p_prev),
+        ]
+
+    def step(self, i):
+        p = self.reduce_p
+        if i == 0:
+            self.begin(p)
+        elif i == 1:
+            self.middle(p, self.rows_p, self.first)
+        elif i == 2:
+            self.end(p, self.rows_p, self.first, self.p_ring, self.free.at[0])
+            for copy in self.scatter:
+                copy.start()
+        elif i == 3:
+            total = self.data[self.own, :]
+            for j, copy in enumerate(self.scatter):
+                copy.wait_recv()
+                total = total + self.second[j]
+            self.data[self.own, :] = total
+            for copy in self.share:
+                copy.start()
+        elif i == 4:
+            for copy in self.scatter:
+                copy.wait_send()
+            for j, copy in enumerate(self.share):
+                copy.wait_recv()
+                self.data[self.origin[j], :] = self.second[7 + j]
+            for copy in self.share:
+                copy.wait_send()
+            self.spread(self.gather_p, self.free.at[0])
+        elif i == 5:
+            self.forward(self.gather_p)
+        elif i == 6:
+            self.settle(self.gather_p)
 
 
 def whole_kernel(cand_ref, orb_ref, panel_out, gram_out, mixing_out,
                  panel, merged, from_core, from_chip, tiles_a, tiles_b, main, mate_a, mate_b,
-                 s00, s01, s02, s10, s11, s12, s20, s21, s22, s30, s31, s32,
-                 work, block, inv, coupling, mixing,
-                 panel_send, panel_recv, send, recv, free, local_sem):
+                 *rest):
+    slots = [rest[3 * u : 3 * u + 3] for u in range(6)]
+    work, block, inv, coupling, mixing, panel_send, panel_recv, send, recv, free, local_sem = rest[18:]
     o = lax.axis_index("orb")
     g = lax.axis_index("grid")
     core = o % 2
@@ -230,40 +309,46 @@
     x_prev = ((x + 3) % RING) * 8 + y * 4 + z
     z_next = x * 8 + y * 4 + (z + 1) % RING
     z_prev = x * 8 + y * 4 + (z + 3) % RING
-    y_mate = x * 8 + (1 - y) * 4 + z
+
+    def at_z(q, flip):
+        return x * 8 + flip * 4 + q
+
+    def at_x(q, flip):
+        return q * 8 + flip * 4 + z
 
     barrier = pltpu.get_barrier_semaphore()
-    for other in (mate, across):
+    near = [mate, across]
+    for other in near:
         pl.semaphore_signal(barrier, inc=1, device_id={"orb": other}, device_id_type=MESH)
-    for other in (x_next, x_prev, z_next, z_prev, y_mate):
+    far = [at_z((z + turn) % RING, (y + flip) % 2) for turn, flip in PEERS]
+    far += [at_x((x + turn) % RING, (y + flip) % 2) for turn, flip in PEERS if turn]
+    for other in far:
         pl.semaphore_signal(barrier, inc=1, device_id={"grid": other}, device_id_type=MESH)
-    pl.semaphore_wait(barrier, 7)
-
-    data = ([tiles_a.at[0], tiles_a.at[1]], [tiles_b.at[0], tiles_b.at[1]],
-            [main.at[0, 0], main.at[0, 1]], [main.at[1, 0], main.at[1, 1]])
-    slots = ((s00, s01, s02), (s10, s11, s12), (s20, s21, s22), (s30, s31, s32))
+    pl.semaphore_wait(barrier, len(near) + len(far))
+
+    data = [[tiles_a.at[0], tiles_a.at[1]], [tiles_b.at[0], tiles_b.at[1]]]
+    data += [[main.at[i, 0], main.at[i, 1]] for i in range(4)]
     units = []
-    for u in range(4):
+    for u in range(6):
+        kind = DirectReduce if u < 2 else RingReduce
         first, second, third = slots[u]
         units.append([
-            HalfReduce(data[u][0], first.at[0], second.at[0], third.at[0], send.at[u, 0], recv.at[u, 0],
-                       free.at[u, 0], x, x_next, x_prev, z, z_next, z_prev, y, y_mate),
-            HalfReduce(data[u][1], first.at[1], second.at[1], third.at[1], send.at[u, 1], recv.at[u, 1],
-                       free.at[u, 1], z, z_next, z_prev, x, x_next, x_prev, y, y_mate),
+            kind(data[u][0], first.at[0], second.at[0], third.at[0], send.at[u, 0], recv.at[u, 0],
+                 free.at[u, 0], x, x_next, x_prev, z, z_next, z_prev, y, at_z),
+            kind(data[u][1], first.at[1], second.at[1], third.at[1], send.at[u, 1], recv.at[u, 1],
+                 free.at[u, 1], z, z_next, z_prev, x, x_next, x_prev, y, at_x),
         ])
-    done = [0] * 4
-
-    def advance(u, upto=None):
-        upto = done[u] + 1 if upto is None else upto
-        while done[u] < upto:
-            for half in units[u]:
-                half.step(done[u])
-            done[u] += 1
+    done = [0] * 6
+
+    def advance(u):
+        for half in units[u]:
+            half.step(done[u])
+        done[u] += 1
 
     quarter = B // 2
 
     def part(t, which, j):
-        return pl.ds(pl.multiple_of(t * B + which * quarter + j * PIECE, PIECE), PIECE)
+        return pl.ds(pl.multiple_of(t * B + j * quarter + which * PIECE, PIECE), PIECE)
 
     def orb_copy(src, dst, other, i):
         return remote(src, dst, panel_send.at[i], panel_recv.at[i], "orb", other)
@@ -277,21 +362,18 @@
     share = {tj: orb_copy(panel.at[mine[tj]], panel.at[mine[tj]], mate, 2 * n + i) for i, tj in enumerate(pieces)}
     for tj in pieces:
         give[tj].start()
-    for i, tj in enumerate(pieces):
+
+    def merge(i):
+        tj = pieces[i]
         give[tj].wait_recv()
         merged[i] = cand_ref[mine[tj], :] + from_core[i]
         cross[tj].start()
 
-    def collect(t):
-        for j in range(PIECES):
-            i = pieces.index((t, j))
-            cross[t, j].wait_recv()
-            panel[mine[t, j], :] = merged[i] + from_chip[i]
-            share[t, j].start()
-
-    def receive(t):
-        for j in range(PIECES):
-            share[t, j].wait_recv()
+    def collect(i):
+        tj = pieces[i]
+        cross[tj].wait_recv()
+        panel[mine[tj], :] = merged[i] + from_chip[i]
+        share[tj].start()
 
     contract = (((1,), (1,)), ((), ()))
 
@@ -301,57 +383,68 @@
     def core_rows(t):
         return panel[pl.ds(pl.multiple_of(t * B + core * quarter, quarter), quarter), :]
 
-    def main_gram(t):
+    def main_gram(i):
         for h in range(2):
-            def column(i, carry, h=h):
-                at = pl.multiple_of(i * 256, 256)
-                main[t, h, :, pl.ds(at, 256)] = product(
-                    panel[t * B : (t + 1) * B, :], orb_ref[pl.ds(h * WIDE + at, 256), :])
+            def column(n, carry, h=h):
+                at = pl.multiple_of(n * 256, 256)
+                main[i, h, :, pl.ds(at, 256)] = product(
+                    panel[i * quarter : (i + 1) * quarter, :], orb_ref[pl.ds(h * WIDE + at, 256), :])
                 return carry
 
             lax.fori_loop(0, WIDE // 256, column, 0)
 
-    collect(0)
-    receive(0)
-    for h in range(2):
-        tiles_a[h] = product(core_rows(0), panel[h * quarter : (h + 1) * quarter, :])
-    advance(0)
-    main_gram(0)
-    advance(0)
-    advance(2)
-    collect(1)
-    advance(0)
-    advance(0)
-    receive(1)
-    advance(0)
-    for h in range(2):
-        columns = panel[B + h * quarter : B + (h + 1) * quarter, :]
-        tiles_b[h, :quarter, :] = product(core_rows(0), columns)
-        tiles_b[h, quarter:, :] = product(core_rows(1), columns)
-    advance(0)
-    advance(1)
-    advance(0)
-    main_gram(1)
-    advance(0)
-    advance(0)
-    advance(0)
-    advance(0)
-    advance(2)
+    def gram_a():
+        for h in range(2):
+            tiles_a[h] = product(core_rows(0), panel[h * quarter : (h + 1) * quarter, :])
+
     save_panel = pltpu.make_async_copy(panel, panel_out, local_sem.at[0])
-    save_panel.start()
+
+    def gram_b():
+        for h in range(2):
+            columns = panel[B + h * quarter : B + (h + 1) * quarter, :]
+            tiles_b[h, :quarter, :] = product(core_rows(0), columns)
+            tiles_b[h, quarter:, :] = product(core_rows(1), columns)
+        save_panel.start()
 
     share_a = [orb_copy(tiles_a.at[h], mate_a.at[h], mate, 3 * n + h) for h in range(2)]
     share_b = [orb_copy(tiles_b.at[h], mate_b.at[h], mate, 3 * n + 2 + h) for h in range(2)]
     scale = 1.0 / CELLS
     own_rows = pl.ds(pl.multiple_of(core * quarter, quarter), quarter)
     mate_rows = pl.ds(pl.multiple_of((1 - core) * quarter, quarter), quarter)
-    for copy in share_a:
-        copy.start()
-    for h in range(2):
-        columns = slice(h * quarter, (h + 1) * quarter)
-        work[own_rows, columns] = tiles_a[h] * scale
-        share_a[h].wait_recv()
-        work[mate_rows, columns] = mate_a[h] * scale
+
+    def start_a():
+        for copy in share_a:
+            copy.start()
+
+    def start_b():
+        for copy in share_b:
+            copy.start()
+
+    def load_a():
+        for h in range(2):
+            columns = slice(h * quarter, (h + 1) * quarter)
+            work[own_rows, columns] = tiles_a[h] * scale
+            share_a[h].wait_recv()
+            work[mate_rows, columns] = mate_a[h] * scale
+
+    def action(name):
+        kind, i = name[:-1], int(name[-1])
+        if kind == "m" or kind == "d":
+            u = 1 + i if kind == "m" else i - 1
+            u = u + 1 if kind == "m" else u
+            now = done[u]
+            done[u] += 1
+            return lambda: [half.step(now) for half in units[u]]
+        table = {
+            "gw": merge, "co": collect, "rc": lambda j: share[pieces[j]].wait_recv(), "g": main_gram,
+            "a": lambda j: gram_a(), "b": lambda j: gram_b(), "xs": lambda j: start_a(),
+            "xw": lambda j: load_a(), "ys": lambda j: start_b(),
+        }
+        return lambda: table[kind](i)
+
+    def perform(names):
+        for name in names:
+            action(name)()
 
     def factor(phase, hooks):
         column = lax.broadcasted_iota(jnp.int32, (BLK, B), 1)
@@ -387,22 +480,17 @@
 
         lax.fori_loop(0, B // BLK, step, 0)
 
-    def schedule(order):
+    def hooks_of(phase):
         hooks = {}
-        spots = [(k, c) for k in range(B // BLK) for c in (0, 4, 8, 12)]
-        for spot, names in zip(spots, order):
-            todo = []
-            for u in names:
-                if done[u] < STEPS:
-                    todo += [(half, done[u]) for half in units[u]]
-                    done[u] += 1
-            if todo:
-                hooks[spot] = lambda todo=todo: [half.step(i) for half, i in todo] and None
+        for (at, k, c), names in BETWEEN.items():
+            if at == phase:
+                todo = [action(name) for name in names]
+                hooks[k, c] = lambda todo=todo: [do() for do in todo] and None
         return hooks
 
-    factor(0, schedule(ORDER_A))
-    for copy in share_b:
-        copy.start()
+    perform(BEFORE)
+    factor(0, hooks_of(0))
+    perform(MIDDLE)
     for h in range(2):
         columns = slice(h * quarter, (h + 1) * quarter)
         coupling[own_rows, columns] = tiles_b[h, :quarter, :] * scale
@@ -418,19 +506,18 @@
         coupling[...], coupling[...], turned, precision=HI, preferred_element_type=jnp.float32)
     coupling[...] = lax.dot_general(
         coupling[...], mixing[:B, :B], turned, precision=HI, preferred_element_type=jnp.float32)
-    factor(1, schedule(ORDER_B))
+    factor(1, hooks_of(1))
     mixing[B:, :B] = -jnp.dot(mixing[B:, B:], coupling[...], precision=HI, preferred_element_type=jnp.float32)
     save_mixing = pltpu.make_async_copy(mixing, mixing_out, local_sem.at[1])
     save_mixing.start()
     saves = [save_panel, save_mixing]
-    while done[2] < STEPS or done[3] < STEPS:
-        for u in (2, 3):
-            if done[u] < STEPS:
-                advance(u)
-    for t in range(2):
+    perform(AFTER)
+    for i in range(4):
+        assert done[2 + i] == RingReduce.steps
         for h in range(2):
             saves.append(pltpu.make_async_copy(
-                main.at[t, h], gram_out.at[pl.ds(t * B, B), pl.ds(h * WIDE, WIDE)], local_sem.at[2 + 2 * t + h]))
+                main.at[i, h], gram_out.at[pl.ds(i * quarter, quarter), pl.ds(h * WIDE, WIDE)],
+                local_sem.at[2 + 2 * i + h]))
             saves[-1].start()
     for copy in [*give.values(), *cross.values(), *share.values(), *share_a, *share_b]:
         copy.wait_send()
@@ -438,9 +525,38 @@
         save.wait()
 
 
-ORDER_A = [(1,), (1,), (2,), (3,), (1,), (1,), (2,), (3,), (1,), (1,), (2,), (1,), (3,), (1,), (1,), (1,)]
-ORDER_B = [(2,), (3,), (2,), (3,), (2,), (3,), (2,), (3,), (2,), (3,), (2,), (3,), (2,), (3,), (2,), (3,)]
-
+BEFORE = [
+    "gw0", "gw1", "gw2", "gw3", "co0", "rc0", "g0", "m0", "co1", "m0", "rc1", "a0",
+    "d1", "g1", "m1", "m0", "d1", "co2", "rc2", "g2", "m1", "m2", "m0", "d1",
+    "co3", "m1", "rc3", "b0", "d2", "g3", "m2", "m3", "m0", "m1", "d1", "d2",
+    "m0", "m2", "m3", "m0", "m1", "d1", "d2", "m2", "m1", "m3", "m0", "d1",
+    "m2", "d2", "m1", "m3", "m0", "d1", "xs0", "xw0", "d2",
+]
+BETWEEN = {
+    (0, 0, 4): ["m1", "m2"],
+    (0, 0, 6): ["m3"],
+    (0, 1, 2): ["m0"],
+    (0, 1, 4): ["m2"],
+    (0, 1, 8): ["d2"],
+    (0, 1, 12): ["m1", "m3"],
+    (0, 2, 0): ["m0"],
+    (0, 2, 4): ["m2"],
+    (0, 2, 6): ["d2", "ys0"],
+    (0, 2, 14): ["m3"],
+    (0, 3, 6): ["m1"],
+    (0, 3, 8): ["m2"],
+    (0, 3, 12): ["m3"],
+    (1, 0, 0): ["m1"],
+    (1, 0, 2): ["m2"],
+    (1, 0, 4): ["m3"],
+    (1, 1, 0): ["m2"],
+    (1, 2, 0): ["m3"],
+    (1, 3, 0): ["m3"],
+}
+MIDDLE = [
+]
+AFTER = [
+]
 
 def whole(cand, orbitals):
     cells = orbitals.shape[1]
@@ -452,7 +568,7 @@
     for rows, columns in UNIT_SHAPES:
         slots += [
             pltpu.VMEM((2, 6, rows // 8, columns), f32),
-            pltpu.VMEM((2, 6, rows // 32, columns), f32),
+            pltpu.VMEM((2, 14, rows // 32, columns), f32),
             pltpu.VMEM((2, 2, rows // 32, columns), f32),
         ]
     return pl.pallas_call(
@@ -471,7 +587,7 @@
             pltpu.VMEM((n, PIECE, cells), bf16),
             pltpu.VMEM((2, 256, 256), f32),
             pltpu.VMEM((2, 512, 256), f32),
-            pltpu.VMEM((2, 2, B, WIDE), f32),
+            pltpu.VMEM((4, 2, B // 2, WIDE), f32),
             pltpu.VMEM((2, 256, 256), f32),
             pltpu.VMEM((2, 512, 256), f32),
             *slots,
@@ -482,10 +598,10 @@
             pltpu.VMEM((ROWS, ROWS), f32),
             pltpu.SemaphoreType.DMA((3 * n + 4,)),
             pltpu.SemaphoreType.DMA((3 * n + 4,)),
-            pltpu.SemaphoreType.DMA((4, 2, COPIES)),
-            pltpu.SemaphoreType.DMA((4, 2, COPIES)),
-            pltpu.SemaphoreType.REGULAR((4, 2, 2)),
-            pltpu.SemaphoreType.DMA((6,)),
+            pltpu.SemaphoreType.DMA((6, 2, COPIES)),
+            pltpu.SemaphoreType.DMA((6, 2, COPIES)),
+            pltpu.SemaphoreType.REGULAR((6, 2, 2)),
+            pltpu.SemaphoreType.DMA((10,)),
         ],
         compiler_params=pltpu.CompilerParams(
             collective_id=0, has_side_effects=True, vmem_limit_bytes=60 << 20),

time: 240 us -> 192 us (0.80)
  Pallas kernels: 203 us -> 155 us
    pallas_call x1, Pallas kernels: 203 us -> 155 us  [whole(): pl.pallas_call(whole_kernel, out_shape=(jax.ShapeDtypeStruct((ROWS, cells...]
where the time goes in v3:
time: 192 us
  Pallas kernels  155 us (81%)
  matrix products  18.3 us (10%)
  other arithmetic  9.41 us (5%)
  between operations  5.97 us (3%)
  local copies, waits for them, and re-layouts  3.01 us (2%)
    pallas_call x1, Pallas kernels, whole(): pl.pallas_call(whole_kernel, out_shape=(jax.ShapeDtypeStruct((ROWS, cells...  155 us
    dot_general x1, matrix products, local(): upper_second = jnp.dot(scaled[B:], gram, precision=lax.Precision.HIGH)  7.37 us
    dot_general x1, matrix products, local(): jnp.dot(scaled[:B, :B], gram[:B], precision=lax.Precision.HIGH)  4.03 us
    concatenate x1, other arithmetic, local(): factor_rows = jnp.concatenate([upper_first, upper_second], 0)  3.98 us

profile of v3, /device:TPU:0, one launch (start us, length us, event | category | flops | bytes accessed | tf_op | source)
XLA Modules:
  0.0 191.9 jit_solution(17760461912872245670)
XLA Ops:
  0.6 1.3 fusion.13
  7.2 0.7 fusion.8
  7.9 2.4 %dynamic-slice_select_fusion.1 = (bf16[512,1536]{1,0:T(8,128)(2,1)S(1)}, bf16[512,1536]{1,0:T(8,128)(2,1)S(1)}) fusion(bf16[2048,1536]{1,0:T(8,128)(2,1)} %orb_ref.1, s32[]{:T(128)S(6)} %select_n.57, pred[]{:T(512)S(6)} %eq.19, s32[]{:T(128)S(6)} %select_n.62, pred[]{:T(512)S(6)} %eq.20), kind=kLoop, calls=%fused_computation.9 | loop fusion | flops 1572864 | bytes 6291466 | tf_op jit(solution)/shard_map/jit(_where)/select_n | solution.py:619
  10.3 1.9 pad_maximum_fusion.1.cand_ref
  12.2 155.2 %shard_map.41 = (bf16[1024,1536]{1,0:T(8,128)(2,1)}, f32[1024,2048]{1,0:T(8,128)}, f32[1024,1024]{1,0:T(8,128)}) custom-call(bf16[1024,1536]{1,0:T(8,128)(2,1)} %pad_maximum_fusion.1.cand_ref, bf16[2048,1536]{1,0:T(8,128)(2,1)} %orb_ref.1), custom_call_target="tpu_custom_call" | custom-call | tf_op jit(solution)/shard_map/pallas_call | solution.py:574
  167.4 0.0 copy-start
  167.4 0.0 copy-start.1
  167.4 3.3 %fusion.6 = f32[256,1536]{1,0:T(8,128)S(1)} fusion(bf16[1024,1536]{1,0:T(8,128)(2,1)} %get-tuple-element.7, f32[1024,1024]{1,0:T(8,128)} %get-tuple-element.5, s32[]{:T(128)S(6)} %select_n.66), kind=kOutput, calls=%fused_computation.14 | convolution fusion | flops 805830656 | bytes 5767172 | tf_op jit(solution)/shard_map/dot_general | solution.py:634
  170.8 0.0 copy-done
  170.8 0.0 slice-start
  170.8 3.5 %convolution_add_fusion = f32[256,1536]{1,0:T(8,128)} fusion(f32[256,1536]{1,0:T(8,128)S(1)} %fusion.6, bf16[1024,1536]{1,0:T(8,128)(2,1)S(1)} %copy-done, f32[1024,1024]{1,0:T(8,128)} %get-tuple-element.5, s32[]{:T(128)S(6)} %select_n.66), kind=kOutput, calls=%fused_computation.5 | convolution fusion | flops 806486016 | bytes 7340036 | tf_op jit(solution)/shard_map/dot_general | solution.py:634
  174.3 0.0 copy-done.1
  174.3 0.0 slice-start.1
  174.3 0.5 broadcast_multiply_fusion
  174.8 0.0 slice-done
  174.8 1.7 slice-done.1
  176.5 7.4 %convolution_select_fusion = f32[512,2048]{1,0:T(8,128)S(1)} fusion(f32[1024,2048]{1,0:T(8,128)S(1)} %bitcast.6, f32[1024,1024]{1,0:T(8,128)S(1)} %broadcast_multiply_fusion, pred[2048]{0:T(1024)(128)(4,1)S(1)} %fusion.8), kind=kOutput, calls=%fused_computation.4 | convolution fusion | flops 6443499520 | bytes 14682112 | tf_op jit(solution)/shard_map/dot_general | solution.py:627
  183.9 4.0 %fusion = f32[512,2048]{1,0:T(8,128)S(1)} fusion(f32[1024,2048]{1,0:T(8,128)S(1)} %bitcast.6, f32[1024,1024]{1,0:T(8,128)S(1)} %broadcast_multiply_fusion), kind=kOutput, calls=%fused_computation.1 | convolution fusion | flops 3221225472 | bytes 9437184 | tf_op jit(solution)/shard_map/dot_general | solution.py:626
  187.9 4.0 %pad_maximum_fusion = f32[1024,2048]{1,0:T(8,128)} fusion(f32[512,2048]{1,0:T(8,128)S(1)} %convolution_select_fusion, f32[512,2048]{1,0:T(8,128)S(1)} %fusion), kind=kLoop, calls=%fused_computation | loop fusion | flops 2097152 | bytes 16777216 | tf_op jit(solution)/shard_map/concatenate | solution.py:629
  (1 shorter events, 0.0 us)
Async XLA Ops:
  167.4 3.4 %copy-start = (bf16[1024,1536]{1,0:T(8,128)(2,1)S(1)}, bf16[1024,1536]{1,0:T(8,128)(2,1)}, u32[]{:S(2)}) copy-start(bf16[1024,1536]{1,0:T(8,128)(2,1)} %get-tuple-element.7) | copy-start | bytes 9437188
  167.4 6.9 %copy-start.1 = (f32[1024,1024]{1,0:T(8,128)S(1)}, f32[1024,1024]{1,0:T(8,128)}, u32[]{:S(2)}) copy-start(f32[1024,1024]{1,0:T(8,128)} %get-tuple-element.5) | copy-start | bytes 12582916
  170.8 4.1 %slice-start = ((s8[8388608]{0:T(1024)(128)(4,1)}), s8[4194304]{0:T(1024)(128)(4,1)S(1)}, s32[]{:S(2)}) async-start(s8[8388608]{0:T(1024)(128)(4,1)} %bitcast.5), calls=%async_computation | async-start | bytes 8388608
  174.3 2.2 %slice-start.1 = ((s8[8388608]{0:T(1024)(128)(4,1)}), s8[4194304]{0:T(1024)(128)(4,1)S(1)}, s32[]{:S(2)}) async-start(s8[8388608]{0:T(1024)(128)(4,1)} %bitcast.5), calls=%async_computation.1 | async-start | bytes 8388608

commit v4 on v3

--- a/solution.py
+++ b/solution.py
@@ -608,32 +608,86 @@
     )(cand, orbitals)
 
 
+def pick_kernel(order_ref, block_ref, out_ref):
+    owner = order_ref[pl.program_id(0)] // BPD == lax.axis_index("orb")
+    out_ref[...] = jnp.where(owner, block_ref[...], jnp.zeros_like(block_ref))
+
+
+def pick(orbitals, block_order):
+    cells = orbitals.shape[1]
+    return pl.pallas_call(
+        pick_kernel,
+        out_shape=jax.ShapeDtypeStruct((ROWS, cells), orbitals.dtype),
+        grid_spec=pltpu.PrefetchScalarGridSpec(
+            num_scalar_prefetch=1,
+            grid=(2,),
+            in_specs=[pl.BlockSpec((B, cells), lambda i, order: (order[i] % BPD, 0))],
+            out_specs=pl.BlockSpec((B, cells), lambda i, order: (i, 0)),
+        ),
+        compiler_params=pltpu.CompilerParams(vmem_limit_bytes=24 << 20),
+    )(block_order, orbitals)
+
+
+PARTS = 4
+
+
+def finish_kernel(order_ref, mixing_ref, gram_ref, panel_ref, factor_ref, ortho_ref, high, low):
+    n = pl.program_id(0)
+    own = lax.axis_index("orb")
+    quarter = ROWS // 4
+    bf16 = jnp.bfloat16
+
+    @pl.when(n == 0)
+    def _():
+        value = mixing_ref[...]
+        high[...] = value.astype(bf16)
+        low[...] = (value - high[...].astype(jnp.float32)).astype(bf16)
+
+    def dot(a, b):
+        return jnp.dot(a, b, preferred_element_type=jnp.float32)
+
+    gram = gram_ref[...]
+    gram_high = gram.astype(bf16)
+    gram_low = (gram - gram_high.astype(jnp.float32)).astype(bf16)
+    keep = jnp.where(own * BPD + n == order_ref[0], 0.0, 1.0 / CELLS)
+    for r in range(4):
+        rows = slice(r * quarter, (r + 1) * quarter)
+        depth = (r + 1) * quarter
+        a, b = high[rows, :depth], low[rows, :depth]
+        total = dot(a, gram_high[:depth]) + (dot(a, gram_low[:depth]) + dot(b, gram_high[:depth]))
+        factor_ref[rows, :] = total * (jnp.float32(1.0 / CELLS) if r < 2 else keep)
+    mine = pl.ds(pl.multiple_of(own * quarter, quarter), quarter)
+    panel = panel_ref[...]
+    ortho_ref[...] = dot(high[mine, :], panel) + dot(low[mine, :], panel)
+
+
+def finish(block_order, mixing, gram, panel):
+    cells = panel.shape[1]
+    f32 = jnp.float32
+    return pl.pallas_call(
+        finish_kernel,
+        out_shape=(jax.ShapeDtypeStruct((ROWS, LOCAL), f32), jax.ShapeDtypeStruct((ROWS // 4, cells), f32)),
+        grid_spec=pltpu.PrefetchScalarGridSpec(
+            num_scalar_prefetch=1,
+            grid=(PARTS,),
+            in_specs=[
+                pl.BlockSpec((ROWS, ROWS), lambda n, order: (0, 0)),
+                pl.BlockSpec((ROWS, LOCAL // PARTS), lambda n, order: (0, n)),
+                pl.BlockSpec((ROWS, cells // PARTS), lambda n, order: (0, n)),
+            ],
+            out_specs=(
+                pl.BlockSpec((ROWS, LOCAL // PARTS), lambda n, order: (0, n)),
+                pl.BlockSpec((ROWS // 4, cells // PARTS), lambda n, order: (0, n)),
+            ),
+            scratch_shapes=[pltpu.VMEM((ROWS, ROWS), jnp.bfloat16)] * 2,
+        ),
+        compiler_params=pltpu.CompilerParams(vmem_limit_bytes=48 << 20),
+    )(block_order, mixing, gram, panel)
+
+
 def local(orbitals, block_order):
-    own_index = lax.axis_index("orb")
-    local_cols = orbitals.shape[0]
-    first_block = block_order[0]
-    second_block = block_order[1]
-
-    def candidate(block_index):
-        piece = lax.dynamic_slice_in_dim(orbitals, block_index % BPD * B, B, 0)
-        return jnp.where(block_index // BPD == own_index, piece, 0).astype(piece.dtype)
-
-    cand = jnp.concatenate([candidate(first_block), candidate(second_block)], 0)
-    panel, gram, mixing = whole(cand, orbitals)
-    scale = jnp.float32(1.0 / CELLS)
-    column_blocks = (own_index * local_cols + jnp.arange(local_cols, dtype=jnp.int32)) // B
-    scaled = mixing * scale
-    upper_first = jnp.dot(scaled[:B, :B], gram[:B], precision=lax.Precision.HIGH)
-    upper_second = jnp.dot(scaled[B:], gram, precision=lax.Precision.HIGH)
-    upper_second = jnp.where((column_blocks == first_block)[None, :], jnp.float32(0.0), upper_second)
-    factor_rows = jnp.concatenate([upper_first, upper_second], 0)
-    rows_dev = ROWS // lax.axis_size("orb")
-    mixing_rows = lax.dynamic_slice_in_dim(mixing, own_index * rows_dev, rows_dev, 0)
-    high = lax.reduce_precision(mixing_rows, 8, 7)
-    low = (mixing_rows - high).astype(jnp.bfloat16)
-    ortho = jnp.dot(high.astype(jnp.bfloat16), panel, preferred_element_type=jnp.float32) + jnp.dot(
-        low, panel, preferred_element_type=jnp.float32)
-    return (factor_rows, ortho)
+    panel, gram, mixing = whole(pick(orbitals, block_order), orbitals)
+    return finish(block_order, mixing, gram, panel)
 
 
 def solution(mesh):

time: 192 us -> 181 us (0.943)
  matrix products: 18.3 us -> 0 us
  Pallas kernels: 155 us -> 173 us
  other arithmetic: 9.41 us -> 0 us
  between operations: 5.97 us -> 0.68 us
  local copies, waits for them, and re-layouts: 3.01 us -> 6.98 us
    pallas_call x0 -> x2, Pallas kernels: none -> 18.3 us  [the longest x1 17.3 us: finish(): pl.pallas_call(finish_kernel, out_shape=(jax.ShapeDtypeStruct((ROWS, LOCA...]
    dot_general x4 -> x0, matrix products: 18.3 us -> none  [the longest x1 7.37 us: local(): upper_second = jnp.dot(scaled[B:], gram, precision=lax.Precision.HIGH)]
    concatenate x2 -> x0, other arithmetic: 5.85 us -> none  [the longest x1 3.98 us: local(): factor_rows = jnp.concatenate([upper_first, upper_second], 0)]
    unnamed x8 -> x10, local copies, waits for them, and re-layouts: 1.7 us -> 6.98 us
    select_n x1 -> x0, other arithmetic: 2.43 us -> none  [candidate(): jnp.where(block_index // BPD == own_index, piece, 0).astype(piece.dtype)]
where the time goes in v4:
time: 181 us
  Pallas kernels  173 us (96%)
  local copies, waits for them, and re-layouts  6.98 us (4%)
    pallas_call x1, Pallas kernels, whole(): pl.pallas_call(whole_kernel, out_shape=(jax.ShapeDtypeStruct((ROWS, cells...  155 us
    pallas_call x1, Pallas kernels, finish(): pl.pallas_call(finish_kernel, out_shape=(jax.ShapeDtypeStruct((ROWS, LOCA...  17.3 us
    unnamed x10, local copies, waits for them, and re-layouts  6.98 us

profile of v4, /device:TPU:0, one launch (start us, length us, event | category | flops | bytes accessed | tf_op | source)
XLA Modules:
  0.0 180.9 jit_solution(5549824543928813406)
XLA Ops:
  0.6 0.0 copy-start
  0.6 2.8 %copy-done = bf16[2048,1536]{1,0:T(8,128)(2,1)S(1)} copy-done((bf16[2048,1536]{1,0:T(8,128)(2,1)S(1)}, bf16[2048,1536]{1,0:T(8,128)(2,1)}, u32[]{:S(2)}) %copy-start) | copy-done | bytes 6291480
  3.4 0.0 copy-start.3
  3.4 0.7 copy-done.3
  4.1 1.0 shard_map.41.cand_ref
  5.1 0.0 copy-start.1
  5.1 1.7 copy-done.1
  6.8 0.0 copy-start.4
  6.8 154.9 %shard_map.42 = (bf16[1024,1536]{1,0:T(8,128)(2,1)}, f32[1024,2048]{1,0:T(8,128)}, f32[1024,1024]{1,0:T(8,128)}) custom-call(bf16[1024,1536]{1,0:T(8,128)(2,1)} %copy-done.1, bf16[2048,1536]{1,0:T(8,128)(2,1)} %orb_ref.1), custom_call_target="tpu_custom_call" | custom-call | tf_op jit(solution)/shard_map/pallas_call | solution.py:574
  161.7 0.0 copy-done.4
  161.7 0.0 copy-start.2
  161.7 1.9 %copy-done.2 = bf16[1024,1536]{1,0:T(8,128)(2,1)S(1)} copy-done((bf16[1024,1536]{1,0:T(8,128)(2,1)S(1)}, bf16[1024,1536]{1,0:T(8,128)(2,1)}, u32[]{:S(2)}) %copy-start.2) | copy-done | bytes 3145752
  163.6 17.3 %shard_map.43 = (f32[1024,2048]{1,0:T(8,128)}, f32[256,1536]{1,0:T(8,128)}) custom-call(s32[16]{0:T(128)S(1)} %copy-done.4, f32[1024,1024]{1,0:T(8,128)} %get-tuple-element.5.mixing_ref, f32[1024,2048]{1,0:T(8,128)} %get-tuple-element.6.gram_ref, bf16[1024,1536]{1,0:T(8,128)(2,1)S(1)} %copy-done.2), custom_call_target="tpu_custom_call" | custom-call | tf_op jit(solution)/shard_map/pallas_call | solution.py:667
Async XLA Ops:
  0.6 2.8 %copy-start = (bf16[2048,1536]{1,0:T(8,128)(2,1)S(1)}, bf16[2048,1536]{1,0:T(8,128)(2,1)}, u32[]{:S(2)}) copy-start(bf16[2048,1536]{1,0:T(8,128)(2,1)} %orb_ref.1) | copy-start | bytes 18874372
  3.4 0.7 copy-start.3
  5.1 1.7 copy-start.1
  6.8 154.9 %copy-start.4 = (s32[16]{0:T(128)S(1)}, s32[16]{0:T(128)}, u32[]{:S(2)}) copy-start(s32[16]{0:T(128)} %order_ref.3) | copy-start | bytes 196
  161.7 1.9 %copy-start.2 = (bf16[1024,1536]{1,0:T(8,128)(2,1)S(1)}, bf16[1024,1536]{1,0:T(8,128)(2,1)}, u32[]{:S(2)}) copy-start(bf16[1024,1536]{1,0:T(8,128)(2,1)} %get-tuple-element.7.panel_ref) | copy-start | bytes 9437188

commit v5 on v4

--- a/solution.py
+++ b/solution.py
@@ -296,7 +296,9 @@
                  panel, merged, from_core, from_chip, tiles_a, tiles_b, main, mate_a, mate_b,
                  *rest):
     slots = [rest[3 * u : 3 * u + 3] for u in range(6)]
-    work, block, inv, coupling, mixing, panel_send, panel_recv, send, recv, free, local_sem = rest[18:]
+    work, block, inv, coupling, mixing, orbitals, panel_send, panel_recv, send, recv, free, local_sem = rest[18:]
+    load = pltpu.make_async_copy(orb_ref, orbitals, local_sem.at[10])
+    load.start()
     o = lax.axis_index("orb")
     g = lax.axis_index("grid")
     core = o % 2
@@ -384,11 +386,13 @@
         return panel[pl.ds(pl.multiple_of(t * B + core * quarter, quarter), quarter), :]
 
     def main_gram(i):
+        if i == 0:
+            load.wait()
         for h in range(2):
             def column(n, carry, h=h):
                 at = pl.multiple_of(n * 256, 256)
                 main[i, h, :, pl.ds(at, 256)] = product(
-                    panel[i * quarter : (i + 1) * quarter, :], orb_ref[pl.ds(h * WIDE + at, 256), :])
+                    panel[i * quarter : (i + 1) * quarter, :], orbitals[pl.ds(h * WIDE + at, 256), :])
                 return carry
 
             lax.fori_loop(0, WIDE // 256, column, 0)
@@ -533,29 +537,26 @@
     "m2", "d2", "m1", "m3", "m0", "d1", "xs0", "xw0", "d2",
 ]
 BETWEEN = {
-    (0, 0, 4): ["m1", "m2"],
-    (0, 0, 6): ["m3"],
-    (0, 1, 2): ["m0"],
-    (0, 1, 4): ["m2"],
-    (0, 1, 8): ["d2"],
-    (0, 1, 12): ["m1", "m3"],
-    (0, 2, 0): ["m0"],
-    (0, 2, 4): ["m2"],
-    (0, 2, 6): ["d2", "ys0"],
-    (0, 2, 14): ["m3"],
-    (0, 3, 6): ["m1"],
-    (0, 3, 8): ["m2"],
+    (0, 0, 10): ["m2", "m1"],
+    (0, 0, 12): ["m3"],
+    (0, 1, 8): ["d2", "m0"],
+    (0, 2, 0): ["d2", "ys0", "m1", "m2"],
+    (0, 2, 4): ["m3"],
+    (0, 3, 0): ["m0"],
     (0, 3, 12): ["m3"],
-    (1, 0, 0): ["m1"],
+    (0, 3, 14): ["m1"],
+    (1, 0, 0): ["m3", "m1"],
     (1, 0, 2): ["m2"],
-    (1, 0, 4): ["m3"],
-    (1, 1, 0): ["m2"],
-    (1, 2, 0): ["m3"],
-    (1, 3, 0): ["m3"],
+    (1, 1, 0): ["m3"],
+    (1, 2, 0): ["m2"],
+    (1, 2, 14): ["m3"],
+    (1, 3, 6): ["m2"],
 }
 MIDDLE = [
+    "m2",
 ]
 AFTER = [
+    "m3",
 ]
 
 def whole(cand, orbitals):
@@ -578,7 +579,7 @@
             jax.ShapeDtypeStruct((ROWS, LOCAL), f32),
             jax.ShapeDtypeStruct((ROWS, ROWS), f32),
         ),
-        in_specs=[pl.BlockSpec(memory_space=pltpu.VMEM)] * 2,
+        in_specs=[pl.BlockSpec(memory_space=pltpu.VMEM), any_space],
         out_specs=(any_space,) * 3,
         scratch_shapes=[
             pltpu.VMEM((ROWS, cells), bf16),
@@ -596,12 +597,13 @@
             pltpu.VMEM((BLK, BLK), f32),
             pltpu.VMEM((B, B), f32),
             pltpu.VMEM((ROWS, ROWS), f32),
+            pltpu.VMEM((LOCAL, cells), bf16),
             pltpu.SemaphoreType.DMA((3 * n + 4,)),
             pltpu.SemaphoreType.DMA((3 * n + 4,)),
             pltpu.SemaphoreType.DMA((6, 2, COPIES)),
             pltpu.SemaphoreType.DMA((6, 2, COPIES)),
             pltpu.SemaphoreType.REGULAR((6, 2, 2)),
-            pltpu.SemaphoreType.DMA((10,)),
+            pltpu.SemaphoreType.DMA((11,)),
         ],
         compiler_params=pltpu.CompilerParams(
             collective_id=0, has_side_effects=True, vmem_limit_bytes=60 << 20),
@@ -624,14 +626,14 @@
             in_specs=[pl.BlockSpec((B, cells), lambda i, order: (order[i] % BPD, 0))],
             out_specs=pl.BlockSpec((B, cells), lambda i, order: (i, 0)),
         ),
-        compiler_params=pltpu.CompilerParams(vmem_limit_bytes=24 << 20),
+        compiler_params=pltpu.CompilerParams(vmem_limit_bytes=60 << 20),
     )(block_order, orbitals)
 
 
 PARTS = 4
 
 
-def finish_kernel(order_ref, mixing_ref, gram_ref, panel_ref, factor_ref, ortho_ref, high, low):
+def finish_kernel(order_ref, mixing_ref, gram_ref, panel_ref, factor_ref, ortho_ref, left, right):
     n = pl.program_id(0)
     own = lax.axis_index("orb")
     quarter = ROWS // 4
@@ -639,26 +641,35 @@
 
     @pl.when(n == 0)
     def _():
-        value = mixing_ref[...]
-        high[...] = value.astype(bf16)
-        low[...] = (value - high[...].astype(jnp.float32)).astype(bf16)
+        for k in range(4):
+            value = mixing_ref[:, k * quarter : (k + 1) * quarter]
+            high = value.astype(bf16)
+            left[:, 3 * k * quarter : (3 * k + 1) * quarter] = high
+            left[:, (3 * k + 1) * quarter : (3 * k + 2) * quarter] = high
+            left[:, (3 * k + 2) * quarter : (3 * k + 3) * quarter] = (value - high.astype(jnp.float32)).astype(bf16)
 
     def dot(a, b):
         return jnp.dot(a, b, preferred_element_type=jnp.float32)
 
-    gram = gram_ref[...]
-    gram_high = gram.astype(bf16)
-    gram_low = (gram - gram_high.astype(jnp.float32)).astype(bf16)
+    for k in range(4):
+        value = gram_ref[k * quarter : (k + 1) * quarter, :]
+        high = value.astype(bf16)
+        right[3 * k * quarter : (3 * k + 1) * quarter, :] = high
+        right[(3 * k + 1) * quarter : (3 * k + 2) * quarter, :] = (value - high.astype(jnp.float32)).astype(bf16)
+        right[(3 * k + 2) * quarter : (3 * k + 3) * quarter, :] = high
     keep = jnp.where(own * BPD + n == order_ref[0], 0.0, 1.0 / CELLS)
     for r in range(4):
         rows = slice(r * quarter, (r + 1) * quarter)
-        depth = (r + 1) * quarter
-        a, b = high[rows, :depth], low[rows, :depth]
-        total = dot(a, gram_high[:depth]) + (dot(a, gram_low[:depth]) + dot(b, gram_high[:depth]))
+        depth = 3 * (r + 1) * quarter
+        total = dot(left[rows, :depth], right[:depth, :])
         factor_ref[rows, :] = total * (jnp.float32(1.0 / CELLS) if r < 2 else keep)
     mine = pl.ds(pl.multiple_of(own * quarter, quarter), quarter)
-    panel = panel_ref[...]
-    ortho_ref[...] = dot(high[mine, :], panel) + dot(low[mine, :], panel)
+    total = jnp.zeros(ortho_ref.shape, jnp.float32)
+    for k in range(4):
+        panel = panel_ref[k * quarter : (k + 1) * quarter, :]
+        for part in (0, 2):
+            total += dot(left[mine, (3 * k + part) * quarter : (3 * k + part + 1) * quarter], panel)
+    ortho_ref[...] = total
 
 
 def finish(block_order, mixing, gram, panel):
@@ -679,9 +690,12 @@
                 pl.BlockSpec((ROWS, LOCAL // PARTS), lambda n, order: (0, n)),
                 pl.BlockSpec((ROWS // 4, cells // PARTS), lambda n, order: (0, n)),
             ),
-            scratch_shapes=[pltpu.VMEM((ROWS, ROWS), jnp.bfloat16)] * 2,
+            scratch_shapes=[
+                pltpu.VMEM((ROWS, 3 * ROWS), jnp.bfloat16),
+                pltpu.VMEM((3 * ROWS, LOCAL // PARTS), jnp.bfloat16),
+            ],
         ),
-        compiler_params=pltpu.CompilerParams(vmem_limit_bytes=48 << 20),
+        compiler_params=pltpu.CompilerParams(vmem_limit_bytes=60 << 20),
     )(block_order, mixing, gram, panel)
 
 

time: 181 us -> 169 us (0.934)
  local copies, waits for them, and re-layouts: 6.98 us -> 0 us
  Pallas kernels: 173 us -> 168 us
    pallas_call x1, Pallas kernels: 155 us -> 147 us  [whole(): pl.pallas_call(whole_kernel, out_shape=(jax.ShapeDtypeStruct((ROWS, cells...]
    unnamed x10 -> x0, local copies, waits for them, and re-layouts: 6.98 us -> none
    pallas_call x1, Pallas kernels: 1.02 us -> 3.96 us  [pick(): pl.pallas_call(pick_kernel, out_shape=jax.ShapeDtypeStruct((ROWS, cells),...]
where the time goes in v5:
time: 169 us
  Pallas kernels  168 us (99%)
    pallas_call x1, Pallas kernels, whole(): pl.pallas_call(whole_kernel, out_shape=(jax.ShapeDtypeStruct((ROWS, cells...  147 us
    pallas_call x1, Pallas kernels, finish(): pl.pallas_call(finish_kernel, out_shape=(jax.ShapeDtypeStruct((ROWS, LOCA...  17.1 us
    pallas_call x1, Pallas kernels, pick(): pl.pallas_call(pick_kernel, out_shape=jax.ShapeDtypeStruct((ROWS, cells),...  3.96 us

profile of v5, /device:TPU:0, one launch (start us, length us, event | category | flops | bytes accessed | tf_op | source)
XLA Modules:
  0.0 169.1 jit_solution(16698755177322480600)
XLA Ops:
  0.6 4.0 %shard_map.41.cand_ref = bf16[1024,1536]{1,0:T(8,128)(2,1)} custom-call(s32[16]{0:T(128)} %order_ref.3, bf16[2048,1536]{1,0:T(8,128)(2,1)} %orb_ref.1), custom_call_target="tpu_custom_call" | custom-call | tf_op jit(solution)/shard_map/pallas_call | solution.py:620
  4.6 147.4 %shard_map.42 = (bf16[1024,1536]{1,0:T(8,128)(2,1)}, f32[1024,2048]{1,0:T(8,128)}, f32[1024,1024]{1,0:T(8,128)}) custom-call(bf16[1024,1536]{1,0:T(8,128)(2,1)} %shard_map.41.cand_ref, bf16[2048,1536]{1,0:T(8,128)(2,1)} %orb_ref.1), custom_call_target="tpu_custom_call" | custom-call | tf_op jit(solution)/shard_map/pallas_call | solution.py:575
  152.0 17.1 %shard_map.43 = (f32[1024,2048]{1,0:T(8,128)}, f32[256,1536]{1,0:T(8,128)}) custom-call(s32[16]{0:T(128)} %order_ref.3, f32[1024,1024]{1,0:T(8,128)} %get-tuple-element.5.mixing_ref, f32[1024,2048]{1,0:T(8,128)} %get-tuple-element.6.gram_ref, bf16[1024,1536]{1,0:T(8,128)(2,1)} %get-tuple-element.7.panel_ref), custom_call_target="tpu_custom_call" | custom-call | tf_op jit(solution)/shard_map/pallas_call | solution.py:678

commit v6 on v5

--- a/solution.py
+++ b/solution.py
@@ -431,6 +431,23 @@
             share_a[h].wait_recv()
             work[mate_rows, columns] = mate_a[h] * scale
 
+    main_saves = [
+        [
+            pltpu.make_async_copy(
+                main.at[i, h], gram_out.at[pl.ds(i * quarter, quarter), pl.ds(h * WIDE, WIDE)],
+                local_sem.at[2 + 2 * i + h])
+            for h in range(2)
+        ]
+        for i in range(4)
+    ]
+
+    def move(u, now):
+        for half in units[u]:
+            half.step(now)
+        if u >= 2 and now == RingReduce.steps - 1:
+            for save in main_saves[u - 2]:
+                save.start()
+
     def action(name):
         kind, i = name[:-1], int(name[-1])
         if kind == "m" or kind == "d":
@@ -438,7 +455,7 @@
             u = u + 1 if kind == "m" else u
             now = done[u]
             done[u] += 1
-            return lambda: [half.step(now) for half in units[u]]
+            return lambda: move(u, now)
         table = {
             "gw": merge, "co": collect, "rc": lambda j: share[pieces[j]].wait_recv(), "g": main_gram,
             "a": lambda j: gram_a(), "b": lambda j: gram_b(), "xs": lambda j: start_a(),
@@ -518,11 +535,7 @@
     perform(AFTER)
     for i in range(4):
         assert done[2 + i] == RingReduce.steps
-        for h in range(2):
-            saves.append(pltpu.make_async_copy(
-                main.at[i, h], gram_out.at[pl.ds(i * quarter, quarter), pl.ds(h * WIDE, WIDE)],
-                local_sem.at[2 + 2 * i + h]))
-            saves[-1].start()
+        saves += main_saves[i]
     for copy in [*give.values(), *cross.values(), *share.values(), *share_a, *share_b]:
         copy.wait_send()
     for save in saves:

time: 169 us -> 167 us (0.988)
    pallas_call x1, Pallas kernels: 147 us -> 146 us  [whole(): pl.pallas_call(whole_kernel, out_shape=(jax.ShapeDtypeStruct((ROWS, cells...]
where the time goes in v6:
time: 167 us
  Pallas kernels  167 us (100%)
    pallas_call x1, Pallas kernels, whole(): pl.pallas_call(whole_kernel, out_shape=(jax.ShapeDtypeStruct((ROWS, cells...  146 us
    pallas_call x1, Pallas kernels, finish(): pl.pallas_call(finish_kernel, out_shape=(jax.ShapeDtypeStruct((ROWS, LOCA...  17.1 us
    pallas_call x1, Pallas kernels, pick(): pl.pallas_call(pick_kernel, out_shape=jax.ShapeDtypeStruct((ROWS, cells),...  3.96 us

profile of v6, /device:TPU:0, one launch (start us, length us, event | category | flops | bytes accessed | tf_op | source)
XLA Modules:
  0.0 167.2 jit_solution(17167289791506595318)
XLA Ops:
  0.6 4.0 %shard_map.41.cand_ref = bf16[1024,1536]{1,0:T(8,128)(2,1)} custom-call(s32[16]{0:T(128)} %order_ref.3, bf16[2048,1536]{1,0:T(8,128)(2,1)} %orb_ref.1), custom_call_target="tpu_custom_call" | custom-call | tf_op jit(solution)/shard_map/pallas_call | solution.py:633
  4.6 145.6 %shard_map.42 = (bf16[1024,1536]{1,0:T(8,128)(2,1)}, f32[1024,2048]{1,0:T(8,128)}, f32[1024,1024]{1,0:T(8,128)}) custom-call(bf16[1024,1536]{1,0:T(8,128)(2,1)} %shard_map.41.cand_ref, bf16[2048,1536]{1,0:T(8,128)(2,1)} %orb_ref.1), custom_call_target="tpu_custom_call" | custom-call | tf_op jit(solution)/shard_map/pallas_call | solution.py:588
  150.2 17.1 %shard_map.43 = (f32[1024,2048]{1,0:T(8,128)}, f32[256,1536]{1,0:T(8,128)}) custom-call(s32[16]{0:T(128)} %order_ref.3, f32[1024,1024]{1,0:T(8,128)} %get-tuple-element.5.mixing_ref, f32[1024,2048]{1,0:T(8,128)} %get-tuple-element.6.gram_ref, bf16[1024,1536]{1,0:T(8,128)(2,1)} %get-tuple-element.7.panel_ref), custom_call_target="tpu_custom_call" | custom-call | tf_op jit(solution)/shard_map/pallas_call | solution.py:691
